TPU v7x, 32 devices: a whole 2x2x4 slice. The times are simulated.
32 devices in a mesh: section: 4 (over y, x), slab: 8 (over z, core).
Axes of the slice: x: 2, y: 2, z: 4, core: 2. Of those that a mesh axis runs over, the one named last changes fastest.
Arguments:
- ref_scan: float32 [256, 256, 512], P('slab', None, 'section'), may hold values from 0.03 to 10, as said below
- def_scan: float32 [256, 256, 512], P('slab', None, 'section'), may hold values from 0.03 to 10, as said below
- offsets: int32 [3, 3, 8, 8, 16], P(None, None, None, None, 'section'), may hold values from -224 to 224, as said below
Outputs:
- subset_shift: float32 [3, 8, 8, 16], P(None, 'slab', None, 'section')
- correlation: float32 [8, 8, 16], P('slab', None, 'section')
- crosslink: float32 [8, 8, 16], P('slab', None, 'section')
Inputs may be any that keep to these rules, and one draw needn't show every extreme that they name: `ref_scan`: positive intensities. `def_scan`: positive intensities. offsets[k, :, s] is subset s's displacement in iteration k, in cells; the cube it points to lies inside the volume; the second and third components lie within -2..2; the slab in which the cube starts, (i * 32 + offsets[k, 0, s]) // 32, is the same in every iteration, and a cube that starts in the last slab starts at its first plane; of the subsets of one device, at most 4 start their cubes in one slab, and exactly 4 do in some slab.
All inputs are finite; a program needn't handle non-finite values.
Results may differ from a plain program's by a relative error of at most 0.0003.
Values may be sent and summed in bfloat16 or wider, within the bound.
A program may use at most 256 MiB of HBM per device.

v0:
```python
import math

import jax
import jax.numpy as jnp
from jax import lax
from jax.sharding import PartitionSpec as P

SUB = 32
RIM = 4
JIT = 2
ITERS = 3


def extended(shard, sides, width):
    for axis, dim in sides:
        peers, length = (lax.axis_size(axis), shard.shape[dim])
        up = [(i, (i + 1) % peers) for i in range(peers - 1)]
        down = [(j, i) for i, j in up]
        last = lax.slice_in_dim(shard, length - width, length, axis=dim)
        first = lax.slice_in_dim(shard, 0, width, axis=dim)
        before = lax.ppermute(last, axis, up)
        after = lax.ppermute(first, axis, down)
        shard = jnp.concatenate([before, shard, after], axis=dim)
    return shard


def from_behind(shard, axis, by):
    peers = lax.axis_size(axis)
    pairs = [(i, i + by) for i in range(peers) if 0 <= i + by < peers]
    return lax.ppermute(shard, axis, pairs)


def tap_tables():
    spots = [float(t) for t in range(-RIM, RIM + 1)]
    bell_curve = [math.exp(-t * t / 4.5) for t in spots]
    bell_total = sum(bell_curve)
    slope_norm = sum([t * t * b for t, b in zip(spots, bell_curve)])
    smooth = [b / bell_total for b in bell_curve]
    slope = [t * b / slope_norm for t, b in zip(spots, bell_curve)]
    return (smooth, slope)


def tap_sum(padded, weights, which_axis, length):
    running = weights[0] * lax.slice_in_dim(padded, 0, length, axis=which_axis)
    for tap_index in range(1, len(weights)):
        running = running + weights[tap_index] * lax.slice_in_dim(
            padded, tap_index, tap_index + length, axis=which_axis
        )
    return running


def zero_pad(values, which_axis):
    widths = [(0, 0)] * values.ndim
    widths[which_axis] = (RIM, RIM)
    return jnp.pad(values, widths)


def solve_three(k_mat, rhs_vec):
    k_zz, k_zy, k_zx = (k_mat[0][0], k_mat[0][1], k_mat[0][2])
    k_yy, k_yx, k_xx = (k_mat[1][1], k_mat[1][2], k_mat[2][2])
    c_zz = k_yy * k_xx - k_yx * k_yx
    c_zy = k_zx * k_yx - k_zy * k_xx
    c_zx = k_zy * k_yx - k_yy * k_zx
    c_yy = k_zz * k_xx - k_zx * k_zx
    c_yx = k_zy * k_zx - k_zz * k_yx
    c_xx = k_zz * k_yy - k_zy * k_zy
    determ = k_zz * c_zz + k_zy * c_zy + k_zx * c_zx
    return [
        (c_zz * rhs_vec[0] + c_zy * rhs_vec[1] + c_zx * rhs_vec[2]) / determ,
        (c_zy * rhs_vec[0] + c_yy * rhs_vec[1] + c_yx * rhs_vec[2]) / determ,
        (c_zx * rhs_vec[0] + c_yx * rhs_vec[1] + c_xx * rhs_vec[2]) / determ,
    ]


def spread_of(centred_sq, cross_vec, k_mat, along, volume):
    square = centred_sq
    for index_a in range(3):
        square = square + 2.0 * cross_vec[index_a] * along[index_a]
        for index_b in range(3):
            square = square + along[index_a] * k_mat[index_a][index_b] * along[index_b]
    return jnp.sqrt(square + 1e-06 * volume)


def gauss_newton(gram_mat, current):
    volume = gram_mat[..., 0, 0]
    mean_val = gram_mat[..., 0, 2] / volume
    mean_grad = [gram_mat[..., 0, 3 + index_a] / volume for index_a in range(3)]
    centred_sq = gram_mat[..., 2, 2] - volume * mean_val * mean_val
    cross_vec = [
        gram_mat[..., 2, 3 + index_a] - volume * mean_val * mean_grad[index_a]
        for index_a in range(3)
    ]
    k_mat = [
        [
            gram_mat[..., 3 + index_a, 3 + index_b]
            - volume * mean_grad[index_a] * mean_grad[index_b]
            + (1e-06 * volume if index_a == index_b else 0.0)
            for index_b in range(3)
        ]
        for index_a in range(3)
    ]
    ref_grad = [
        gram_mat[..., 1, 3 + index_a] - mean_grad[index_a] * gram_mat[..., 0, 1]
        for index_a in range(3)
    ]
    spread_now = spread_of(centred_sq, cross_vec, k_mat, current, volume)
    first_part = solve_three(k_mat, ref_grad)
    second_part = solve_three(k_mat, cross_vec)
    newest = [spread_now * first_part[index_a] - second_part[index_a] for index_a in range(3)]
    return (newest, (mean_val, centred_sq, cross_vec, k_mat, ref_grad, volume))


def finish(gram_mat, newest, moment_set, ref_mean):
    mean_val, centred_sq, cross_vec, k_mat, ref_grad, volume = moment_set
    spread_new = spread_of(centred_sq, cross_vec, k_mat, newest, volume)
    score_sum = gram_mat[..., 1, 2] - mean_val * gram_mat[..., 0, 1]
    for index_a in range(3):
        score_sum = score_sum + ref_grad[index_a] * newest[index_a]
    correlation = score_sum / spread_new
    polymer = mean_val / (mean_val + ref_mean)
    crosslink = (
        -1000.0
        * (jnp.log(1.0 - polymer) + polymer + 0.4 * polymer * polymer)
        / (106.3 * (jnp.cbrt(polymer) - 0.5 * polymer))
    )
    return (correlation, crosslink)


def slot_plan(route_table, owners, slot_rank, holder, capacity, sub_x):
    slabs, subsets = owners.shape
    hit_mask = (
        (owners == holder)[:, None, :]
        & (slot_rank[:, None, :] == jnp.arange(capacity, dtype=jnp.int32)[None, :, None])
    ).astype(jnp.int32)
    is_valid = jnp.sum(hit_mask, axis=2) > 0
    picked = jnp.sum(hit_mask[None, None] * route_table[:, :, :, None, :], axis=4)
    index_j = jnp.arange(subsets, dtype=jnp.int32)
    row_pos = jnp.sum(hit_mask * (index_j // sub_x)[None, None, :], axis=2) * SUB
    col_pos = jnp.sum(hit_mask * (index_j % sub_x)[None, None, :], axis=2) * SUB
    home_z = (jnp.arange(slabs, dtype=jnp.int32) * SUB)[None, :, None]
    z_start = jnp.where(is_valid[None], home_z + picked[:, 0] - holder * SUB, 0)
    y_start = jnp.where(is_valid[None], row_pos[None] + picked[:, 1], 0)
    x_start = jnp.where(is_valid[None], col_pos[None] + picked[:, 2], 0) + JIT
    return (z_start, y_start, x_start)


def gram_from(window, placed, inside):
    highest = lax.Precision.HIGHEST
    count = jnp.sum(inside) * (SUB * SUB)
    ref_total = jnp.sum(placed)
    field_total = jnp.sum(window, axis=1)
    ref_square = jnp.dot(placed, placed, precision=highest, preferred_element_type=jnp.float32)
    cross_ref = jnp.dot(window, placed, precision=highest, preferred_element_type=jnp.float32)
    cross_field = jnp.dot(window, window.T, precision=highest, preferred_element_type=jnp.float32)
    top_row = jnp.concatenate([jnp.stack([count, ref_total]), field_total])
    second_row = jnp.concatenate([jnp.stack([ref_total, ref_square]), cross_ref])
    lower_rows = jnp.concatenate([field_total[:, None], cross_ref[:, None], cross_field], axis=1)
    return jnp.concatenate([top_row[None], second_row[None], lower_rows], axis=0)


def slot_grams(source, arrived, z_start, y_start, x_start):
    slabs, capacity, volume = arrived.shape
    per_turn = 4
    group_size = per_turn * capacity
    slot_total = slabs * capacity

    def one_whole(ref_block, z_first, y_first, x_first):
        placed = ref_block.astype(jnp.float32)
        window = lax.dynamic_slice(
            source, (0, z_first, y_first, x_first), (4, SUB, SUB, SUB)
        ).reshape(4, volume)
        return gram_from(window, placed, jnp.ones((SUB,), jnp.float32))

    def per_group(bundle):
        return jax.vmap(one_whole)(bundle[0], bundle[1], bundle[2], bundle[3])

    bundle = (
        arrived.reshape(slot_total // group_size, group_size, volume),
        z_start.reshape(-1, group_size),
        y_start.reshape(-1, group_size),
        x_start.reshape(-1, group_size),
    )
    gram_set = lax.map(per_group, bundle)
    return gram_set.reshape(slabs, capacity, 6, 6)


def body(ref_scan, def_scan, offsets):
    smooth, slope = tap_tables()
    slabs = lax.axis_size("slab")
    me_slab = lax.axis_index("slab")
    planes, rows_all, cols_dev = ref_scan.shape
    scan_pair = jnp.stack([ref_scan, def_scan])
    grown = extended(scan_pair, (("section", 3), ("slab", 1)), RIM)
    ref_x = tap_sum(grown[0], smooth, 2, cols_dev)
    def_gx = tap_sum(grown[1], smooth, 2, cols_dev)
    def_dx = tap_sum(grown[1], slope, 2, cols_dev)
    ref_xy = tap_sum(zero_pad(ref_x, 1), smooth, 1, rows_all)
    gx_pad = zero_pad(def_gx, 1)
    def_gg = tap_sum(gx_pad, smooth, 1, rows_all)
    def_dg = tap_sum(gx_pad, slope, 1, rows_all)
    def_gd = tap_sum(zero_pad(def_dx, 1), smooth, 1, rows_all)
    smoothed = tap_sum(ref_xy, smooth, 0, planes)
    fields = jnp.stack(
        [
            tap_sum(def_gg, smooth, 0, planes),
            tap_sum(def_gg, slope, 0, planes),
            tap_sum(def_dg, smooth, 0, planes),
            tap_sum(def_gd, smooth, 0, planes),
        ]
    )
    fields_wide = extended(fields, (("section", 3),), JIT)
    sub_y = rows_all // SUB
    sub_x = cols_dev // SUB
    subsets = sub_y * sub_x
    volume = SUB * SUB * SUB
    blocks = (
        smoothed.reshape(SUB, sub_y, SUB, sub_x, SUB)
        .transpose(1, 3, 0, 2, 4)
        .reshape(subsets, volume)
    )
    ref_mean = jnp.mean(blocks, axis=1)
    centred = blocks - ref_mean[:, None]
    normed = (
        centred / jnp.sqrt(jnp.sum(centred * centred, axis=1) + 1e-06 * volume)[:, None]
    ).astype(jnp.bfloat16)
    route_table = offsets.reshape(ITERS, 3, slabs, subsets)
    owners = (jnp.arange(slabs, dtype=jnp.int32)[:, None] * SUB + route_table[0, 0]) // SUB
    earlier = (
        jnp.arange(subsets, dtype=jnp.int32)[:, None]
        > jnp.arange(subsets, dtype=jnp.int32)[None, :]
    )
    same_slab = owners[:, :, None] == owners[:, None, :]
    slot_rank = jnp.sum(same_slab & earlier[None], axis=2)
    capacity = max(2, (subsets + slabs - 1) // slabs)
    my_owner = lax.dynamic_index_in_dim(owners, me_slab, 0, keepdims=False)
    my_rank = lax.dynamic_index_in_dim(slot_rank, me_slab, 0, keepdims=False)
    outgoing = jnp.zeros((slabs, capacity, volume), jnp.bfloat16).at[my_owner, my_rank].set(normed)
    arrived = lax.all_to_all(outgoing, "slab", split_axis=0, concat_axis=0, tiled=True)
    plan_own = slot_plan(route_table, owners, slot_rank, me_slab, capacity, sub_x)
    beyond = from_behind(fields_wide, "slab", -1)
    tall = jnp.concatenate([fields_wide, beyond], axis=1)
    my_table = lax.dynamic_index_in_dim(route_table, me_slab, 2, keepdims=False).astype(jnp.float32)
    current = [jnp.zeros((subsets,), jnp.float32) for index_a in range(3)]
    for turn_index in range(ITERS):
        slot_sums = slot_grams(
            tall, arrived, plan_own[0][turn_index], plan_own[1][turn_index], plan_own[2][turn_index]
        )
        returned = lax.all_to_all(slot_sums, "slab", split_axis=0, concat_axis=0, tiled=True)
        my_grams = returned[my_owner, my_rank]
        newest, moment_set = gauss_newton(my_grams, current)
        if turn_index + 1 < ITERS:
            current = [
                newest[index_a] + my_table[turn_index, index_a] - my_table[turn_index + 1, index_a]
                for index_a in range(3)
            ]
    correlation, crosslink = finish(my_grams, newest, moment_set, ref_mean)
    subset_shift = jnp.stack(newest).reshape(3, 1, sub_y, sub_x)
    return (subset_shift, correlation.reshape(1, sub_y, sub_x), crosslink.reshape(1, sub_y, sub_x))


def solution(mesh):
    in_specs = (
        P("slab", None, "section"),
        P("slab", None, "section"),
        P(None, None, None, None, "section"),
    )
    out_specs = (
        P(None, "slab", None, "section"),
        P("slab", None, "section"),
        P("slab", None, "section"),
    )
    return jax.shard_map(body, mesh=mesh, in_specs=in_specs, out_specs=out_specs, check_vma=False)
```

profile of v0, /device:TPU:0, one launch (start us, length us, event | category | flops | bytes accessed | tf_op | source)
XLA Modules:
  0.0 1837.7 jit_solution(16771195192307919602)
XLA Ops:
  33.5 7.0 pad_maximum_fusion.8
  40.5 7.3 slice_bitcast_fusion
  47.8 7.9 multiply_add_fusion.3
  55.7 12.4 fusion.42
  68.1 44.0 %multiply_add_fusion.2 = (f32[40,256,128]{1,0,2:T(8,128)}, f32[40,256,128]{1,0,2:T(8,128)}) fusion(f32[40,256,128]{1,0,2:T(8,128)} %get-tuple-element.592), kind=kLoop, calls=%fused_computation.154 | loop fusion | flops 44564480 | bytes 15728640 | tf_op jit(solution)/shard_map/add | solution.py:46
  112.1 26.0 %add_bitcast_fusion.1 = (f32[1,32,256,128]{2,1,3,0:T(8,128)}, f32[1,32,256,128]{2,1,3,0:T(8,128)}) fusion(f32[40,256,128]{1,0,2:T(8,128)} %get-tuple-element.596), kind=kLoop, calls=%fused_computation.210 | loop fusion | flops 35651584 | bytes 46137344 | tf_op jit(solution)/shard_map/stack | solution.py:203
  138.1 26.8 %fusion.59 = (f32[1,32,256,128]{2,1,3,0:T(8,128)}, f32[1,32,256,128]{2,1,3,0:T(8,128)}) fusion(f32[40,256,128]{1,0,2:T(8,128)S(1)} %bitcast.365, f32[40,256,128]{1,0,2:T(8,128)} %get-tuple-element.597), kind=kLoop, calls=%fused_computation.158 | loop fusion | flops 35651584 | bytes 83886080 | tf_op jit(solution)/shard_map/stack | solution.py:203
  167.8 6.9 collective-permute-start.4
  178.6 6.6 pad_maximum_fusion.7
  187.6 18.7 %fusion.50 = f32[40,256,128]{1,0,2:T(8,128)} fusion(f32[40,256,136]{1,0,2:T(8,128)} %get-tuple-element.587), kind=kLoop, calls=%fused_computation.136 | loop fusion | flops 22282240 | bytes 52428800 | tf_op jit(solution)/shard_map/add | solution.py:46
  206.3 26.5 %fusion.26 = f32[40,256,128]{1,0,2:T(8,128)S(1)} fusion(f32[40,256,128]{1,0,2:T(8,128)} %fusion.50), kind=kLoop, calls=%fused_computation.111 | loop fusion | flops 22282240 | bytes 10485760 | tf_op jit(solution)/shard_map/add | solution.py:46
  238.7 11.0 reshape.5925
  249.7 17.6 copy.282
  267.3 11.8 reshape.5926
  279.1 7.0 bitcast_reduce_fusion
  286.9 8.2 multiply_reduce_fusion
  299.6 41.6 %scatter_fusion = bf16[8,4,32768]{2,1,0:T(4,128)(2,1)} fusion(bf16[8,4,32768]{2,1,0:T(4,128)(2,1)} %broadcast_in_dim.169, s32[32]{0:T(128)S(1)} %get-tuple-element.604, bf16[32,32768]{1,0:T(8,128)(2,1)S(1)} %divide_convert_fusion), kind=kCustom, calls=%fused_computation.3 | custom fusion | bytes 6291712 | tf_op jit(solution)/shard_map/scatter | solution.py:237
  341.2 23.8 %all-to-all-start = ((bf16[8,4,32768]{2,1,0:T(4,128)(2,1)}), bf16[8,4,32768]{2,1,0:T(4,128)(2,1)}, u32[]{:S(2)}, u32[]{:S(2)}) async-start(bf16[8,4,32768]{2,1,0:T(4,128)(2,1)} %scatter_fusion), calls=%async_computation | async-start | bytes 4194304 | tf_op jit(solution)/shard_map/all_to_all | solution.py:238
  383.3 51.9 %all-to-all-done = bf16[8,4,32768]{2,1,0:T(4,128)(2,1)} async-done(((bf16[8,4,32768]{2,1,0:T(4,128)(2,1)}), bf16[8,4,32768]{2,1,0:T(4,128)(2,1)}, u32[]{:S(2)}, u32[]{:S(2)}) %all-to-all-start) | async-done | bytes 2097184 | tf_op jit(solution)/shard_map/all_to_all | solution.py:238
  437.8 24.5 %pad_maximum_fusion.6 = f32[4,64,256,132]{2,1,3,0:T(8,128)} fusion(f32[4,32,256,132]{2,1,3,0:T(8,128)} %collective-permute-done.6, f32[4,32,256,2]{2,1,3,0:T(8,128)S(1)} %collective-permute-done.5, f32[1,32,256,128]{2,1,3,0:T(8,128)} %get-tuple-element.625, f32[1,32,256,128]{2,1,3,0:T(8,128)} %get-tuple-element.626, ...), kind=kLoop, calls=%fused_computation.73 | loop fusion | flops 51904512 | bytes 69206016 | tf_op jit(solution)/shard_map/concatenate | solution.py:241
  462.3 68.8 %copy.287 = f32[4,64,256,132]{3,2,1,0:T(8,128)} copy(f32[4,64,256,132]{2,1,3,0:T(8,128)} %pad_maximum_fusion.6) | data formatting | bytes 69206016 | tf_op jit(solution)/shard_map/while | solution.py:183
  531.2 419.8 %while.43 = (s32[]{:T(128)}, f32[2,16,6,6]{1,0,3,2:T(2,128)S(1)}, bf16[2,16,32768]{2,1,0:T(8,128)(2,1)S(1)}, s32[2,16]{1,0:T(2,128)S(1)}, s32[2,16]{1,0:T(2,128)...) while((s32[]{:T(128)}, f32[2,16,6,6]{1,0,3,2:T(2,128)S(1)}, ...), condition=%wide.region_11.12_spmd, body=%wide.region_8.11_spmd.sunk | while | flops 130025904 | bytes 50360332 | solution.py:183
  531.6 113.1 %while.48 = (s32[]{:T(128)}, f32[4,64,256,132]{3,2,1,0:T(8,128)}, s32[16,4]{0,1:T(4,128)S(1)}, f32[16,4,32,32,32]{4,3,2,1,0:T(8,128)}, s32[]{:T(128)}) while((s32[]{:T(128)}, f32[4,64,256,132]{3,2,1,0:T(8,128)}, s32[16,4]{0,1:T(4,128)S(1)}, f32[16,4,32,32,32]{4,3,2,1,0:T(8,128)}, s32[]{:T(128)}) %tuple.285), condition=%wide.while_cond, body=%wide.while_body.sunk | while | flops 2 | bytes 4195973 | solution.py:169
  574.8 6.5 bitcast_dynamic-update-slice_fusion.8
  631.2 6.5 bitcast_dynamic-update-slice_fusion.8
  644.8 24.3 %reshape.6268 = f32[16,4,32768]{2,1,0:T(4,128)} reshape(f32[16,4,32,32,32]{4,3,2,1,0:T(8,128)} %get-tuple-element.855) | data formatting | bytes 16777216 | tf_op jit(solution)/shard_map/while/body/eval_jaxpr/vmap()/reshape | solution.py:171
  669.1 37.4 %fusion.309 = f32[16,4,4]{2,1,0:T(4,128)S(1)} fusion(f32[16,4,32768]{2,1,0:T(4,128)} %reshape.6268), kind=kOutput, calls=%fused_computation.611.clone.1 | convolution fusion | flops 100663296 | bytes 8389632 | tf_op jit(solution)/shard_map/while/body/eval_jaxpr/vmap()/dot_general | solution.py:154
  706.6 20.6 %fusion.310 = f32[16,1,4]{2,1,0:T(1,128)S(1)} fusion(f32[16,4,32768]{2,1,0:T(4,128)} %reshape.6268, bf16[16,32768,1]{1,0,2:T(8,128)(2,1)S(1)} %dynamic-slice_bitcast_fusion.6), kind=kOutput, calls=%fused_computation.13.clone.1 | convolution fusion | flops 25165824 | bytes 9437440 | tf_op jit(solution)/shard_map/while/body/eval_jaxpr/vmap()/dot_general | solution.py:153
  727.3 12.5 reduce_sum.171
  741.2 113.4 %while.48 = (s32[]{:T(128)}, f32[4,64,256,132]{3,2,1,0:T(8,128)}, s32[16,4]{0,1:T(4,128)S(1)}, f32[16,4,32,32,32]{4,3,2,1,0:T(8,128)}, s32[]{:T(128)}) while((s32[]{:T(128)}, f32[4,64,256,132]{3,2,1,0:T(8,128)}, s32[16,4]{0,1:T(4,128)S(1)}, f32[16,4,32,32,32]{4,3,2,1,0:T(8,128)}, s32[]{:T(128)}) %tuple.285), condition=%wide.while_cond, body=%wide.while_body.sunk | while | flops 2 | bytes 4195973 | solution.py:169
  784.4 6.5 bitcast_dynamic-update-slice_fusion.8
  841.1 6.5 bitcast_dynamic-update-slice_fusion.8
  854.6 24.3 %reshape.6268 = f32[16,4,32768]{2,1,0:T(4,128)} reshape(f32[16,4,32,32,32]{4,3,2,1,0:T(8,128)} %get-tuple-element.855) | data formatting | bytes 16777216 | tf_op jit(solution)/shard_map/while/body/eval_jaxpr/vmap()/reshape | solution.py:171
  878.9 37.4 %fusion.309 = f32[16,4,4]{2,1,0:T(4,128)S(1)} fusion(f32[16,4,32768]{2,1,0:T(4,128)} %reshape.6268), kind=kOutput, calls=%fused_computation.611.clone.1 | convolution fusion | flops 100663296 | bytes 8389632 | tf_op jit(solution)/shard_map/while/body/eval_jaxpr/vmap()/dot_general | solution.py:154
  916.4 20.6 %fusion.310 = f32[16,1,4]{2,1,0:T(1,128)S(1)} fusion(f32[16,4,32768]{2,1,0:T(4,128)} %reshape.6268, bf16[16,32768,1]{1,0,2:T(8,128)(2,1)S(1)} %dynamic-slice_bitcast_fusion.6), kind=kOutput, calls=%fused_computation.13.clone.1 | convolution fusion | flops 25165824 | bytes 9437440 | tf_op jit(solution)/shard_map/while/body/eval_jaxpr/vmap()/dot_general | solution.py:153
  937.2 12.5 reduce_sum.171
  956.3 417.2 %while.45 = (s32[]{:T(128)}, f32[2,16,6,6]{1,0,3,2:T(2,128)S(1)}, bf16[2,16,32768]{2,1,0:T(8,128)(2,1)S(1)}, s32[2,16]{1,0:T(2,128)S(1)}, s32[2,16]{1,0:T(2,128)...) while((s32[]{:T(128)}, f32[2,16,6,6]{1,0,3,2:T(2,128)S(1)}, ...), condition=%wide.region_15.16_spmd, body=%wide.region_12.15_spmd.sunk | while | flops 130025904 | bytes 50360332 | solution.py:183
  956.5 111.8 %while.49 = (s32[]{:T(128)}, f32[4,64,256,132]{3,2,1,0:T(8,128)}, s32[16,4]{0,1:T(4,128)S(1)}, f32[16,4,32,32,32]{4,3,2,1,0:T(8,128)}, s32[]{:T(128)}) while((s32[]{:T(128)}, f32[4,64,256,132]{3,2,1,0:T(8,128)}, s32[16,4]{0,1:T(4,128)S(1)}, f32[16,4,32,32,32]{4,3,2,1,0:T(8,128)}, s32[]{:T(128)}) %tuple.282), condition=%wide.while_cond.1, body=%wide.while_body.1.sunk | while | flops 2 | bytes 4195973 | solution.py:169
  1068.3 24.3 %reshape.6269 = f32[16,4,32768]{2,1,0:T(4,128)} reshape(f32[16,4,32,32,32]{4,3,2,1,0:T(8,128)} %get-tuple-element.868) | data formatting | bytes 16777216 | tf_op jit(solution)/shard_map/while/body/eval_jaxpr/vmap()/reshape | solution.py:171
  1092.6 37.4 %fusion.315 = f32[16,4,4]{2,1,0:T(4,128)S(1)} fusion(f32[16,4,32768]{2,1,0:T(4,128)} %reshape.6269), kind=kOutput, calls=%fused_computation.612.clone.1 | convolution fusion | flops 100663296 | bytes 8389632 | tf_op jit(solution)/shard_map/while/body/eval_jaxpr/vmap()/dot_general | solution.py:154
  1130.1 20.6 %fusion.316 = f32[16,1,4]{2,1,0:T(1,128)S(1)} fusion(f32[16,4,32768]{2,1,0:T(4,128)} %reshape.6269, bf16[16,32768,1]{1,0,2:T(8,128)(2,1)S(1)} %dynamic-slice_bitcast_fusion.7), kind=kOutput, calls=%fused_computation.34.clone.1 | convolution fusion | flops 25165824 | bytes 9437440 | tf_op jit(solution)/shard_map/while/body/eval_jaxpr/vmap()/dot_general | solution.py:153
  1150.9 12.5 reduce_sum.173
  1164.8 112.4 %while.49 = (s32[]{:T(128)}, f32[4,64,256,132]{3,2,1,0:T(8,128)}, s32[16,4]{0,1:T(4,128)S(1)}, f32[16,4,32,32,32]{4,3,2,1,0:T(8,128)}, s32[]{:T(128)}) while((s32[]{:T(128)}, f32[4,64,256,132]{3,2,1,0:T(8,128)}, s32[16,4]{0,1:T(4,128)S(1)}, f32[16,4,32,32,32]{4,3,2,1,0:T(8,128)}, s32[]{:T(128)}) %tuple.282), condition=%wide.while_cond.1, body=%wide.while_body.1.sunk | while | flops 2 | bytes 4195973 | solution.py:169
  1277.1 24.3 %reshape.6269 = f32[16,4,32768]{2,1,0:T(4,128)} reshape(f32[16,4,32,32,32]{4,3,2,1,0:T(8,128)} %get-tuple-element.868) | data formatting | bytes 16777216 | tf_op jit(solution)/shard_map/while/body/eval_jaxpr/vmap()/reshape | solution.py:171
  1301.4 37.4 %fusion.315 = f32[16,4,4]{2,1,0:T(4,128)S(1)} fusion(f32[16,4,32768]{2,1,0:T(4,128)} %reshape.6269), kind=kOutput, calls=%fused_computation.612.clone.1 | convolution fusion | flops 100663296 | bytes 8389632 | tf_op jit(solution)/shard_map/while/body/eval_jaxpr/vmap()/dot_general | solution.py:154
  1338.9 20.6 %fusion.316 = f32[16,1,4]{2,1,0:T(1,128)S(1)} fusion(f32[16,4,32768]{2,1,0:T(4,128)} %reshape.6269, bf16[16,32768,1]{1,0,2:T(8,128)(2,1)S(1)} %dynamic-slice_bitcast_fusion.7), kind=kOutput, calls=%fused_computation.34.clone.1 | convolution fusion | flops 25165824 | bytes 9437440 | tf_op jit(solution)/shard_map/while/body/eval_jaxpr/vmap()/dot_general | solution.py:153
  1359.7 12.5 reduce_sum.173
  1374.1 420.2 %while.47 = (s32[]{:T(128)}, f32[2,16,6,6]{1,0,3,2:T(2,128)S(1)}, bf16[2,16,32768]{2,1,0:T(8,128)(2,1)S(1)}, s32[2,16]{1,0:T(2,128)S(1)}, s32[2,16]{1,0:T(2,128)...) while((s32[]{:T(128)}, f32[2,16,6,6]{1,0,3,2:T(2,128)S(1)}, ...), condition=%wide.region_19.20_spmd, body=%wide.region_16.19_spmd.sunk | while | flops 130025904 | bytes 50360332 | solution.py:183
  1374.4 113.2 %while.50 = (s32[]{:T(128)}, f32[4,64,256,132]{3,2,1,0:T(8,128)}, s32[16,4]{0,1:T(4,128)S(1)}, f32[16,4,32,32,32]{4,3,2,1,0:T(8,128)}, s32[]{:T(128)}) while((s32[]{:T(128)}, f32[4,64,256,132]{3,2,1,0:T(8,128)}, s32[16,4]{0,1:T(4,128)S(1)}, f32[16,4,32,32,32]{4,3,2,1,0:T(8,128)}, s32[]{:T(128)}) %tuple.279), condition=%wide.while_cond.2, body=%wide.while_body.2.sunk | while | flops 2 | bytes 4195973 | solution.py:169
  1417.6 6.5 bitcast_dynamic-update-slice_fusion.6
  1474.4 6.5 bitcast_dynamic-update-slice_fusion.6
  1487.6 24.3 %reshape.6270 = f32[16,4,32768]{2,1,0:T(4,128)} reshape(f32[16,4,32,32,32]{4,3,2,1,0:T(8,128)} %get-tuple-element.881) | data formatting | bytes 16777216 | tf_op jit(solution)/shard_map/while/body/eval_jaxpr/vmap()/reshape | solution.py:171
  1511.9 37.4 %fusion.321 = f32[16,4,4]{2,1,0:T(4,128)S(1)} fusion(f32[16,4,32768]{2,1,0:T(4,128)} %reshape.6270), kind=kOutput, calls=%fused_computation.613.clone.1 | convolution fusion | flops 100663296 | bytes 8389632 | tf_op jit(solution)/shard_map/while/body/eval_jaxpr/vmap()/dot_general | solution.py:154
  1549.4 20.6 %fusion.322 = f32[16,1,4]{2,1,0:T(1,128)S(1)} fusion(f32[16,4,32768]{2,1,0:T(4,128)} %reshape.6270, bf16[16,32768,1]{1,0,2:T(8,128)(2,1)S(1)} %dynamic-slice_bitcast_fusion.8), kind=kOutput, calls=%fused_computation.55.clone.1 | convolution fusion | flops 25165824 | bytes 9437440 | tf_op jit(solution)/shard_map/while/body/eval_jaxpr/vmap()/dot_general | solution.py:153
  1570.2 12.5 reduce_sum.175
  1584.0 113.6 %while.50 = (s32[]{:T(128)}, f32[4,64,256,132]{3,2,1,0:T(8,128)}, s32[16,4]{0,1:T(4,128)S(1)}, f32[16,4,32,32,32]{4,3,2,1,0:T(8,128)}, s32[]{:T(128)}) while((s32[]{:T(128)}, f32[4,64,256,132]{3,2,1,0:T(8,128)}, s32[16,4]{0,1:T(4,128)S(1)}, f32[16,4,32,32,32]{4,3,2,1,0:T(8,128)}, s32[]{:T(128)}) %tuple.279), condition=%wide.while_cond.2, body=%wide.while_body.2.sunk | while | flops 2 | bytes 4195973 | solution.py:169
  1620.2 6.5 bitcast_dynamic-update-slice_fusion.6
  1627.4 6.5 bitcast_dynamic-update-slice_fusion.6
  1677.0 6.5 bitcast_dynamic-update-slice_fusion.6
  1684.1 6.5 bitcast_dynamic-update-slice_fusion.6
  1697.7 24.3 %reshape.6270 = f32[16,4,32768]{2,1,0:T(4,128)} reshape(f32[16,4,32,32,32]{4,3,2,1,0:T(8,128)} %get-tuple-element.881) | data formatting | bytes 16777216 | tf_op jit(solution)/shard_map/while/body/eval_jaxpr/vmap()/reshape | solution.py:171
  1722.0 37.4 %fusion.321 = f32[16,4,4]{2,1,0:T(4,128)S(1)} fusion(f32[16,4,32768]{2,1,0:T(4,128)} %reshape.6270), kind=kOutput, calls=%fused_computation.613.clone.1 | convolution fusion | flops 100663296 | bytes 8389632 | tf_op jit(solution)/shard_map/while/body/eval_jaxpr/vmap()/dot_general | solution.py:154
  1759.5 20.6 %fusion.322 = f32[16,1,4]{2,1,0:T(1,128)S(1)} fusion(f32[16,4,32768]{2,1,0:T(4,128)} %reshape.6270, bf16[16,32768,1]{1,0,2:T(8,128)(2,1)S(1)} %dynamic-slice_bitcast_fusion.8), kind=kOutput, calls=%fused_computation.55.clone.1 | convolution fusion | flops 25165824 | bytes 9437440 | tf_op jit(solution)/shard_map/while/body/eval_jaxpr/vmap()/dot_general | solution.py:153
  1780.2 12.5 reduce_sum.175
  (743 shorter events, 743.4 us)
Async XLA Ops:
  11.6 13.9 copy-start.2
  11.6 13.9 copy-start.3
  12.9 12.2 collective-permute-start.1
  14.5 11.0 collective-permute-start
  26.1 4.6 collective-permute-start.3
  27.7 5.4 collective-permute-start.2
  68.1 70.0 %slice-start = ((s8[5242880]{0:T(1024)(128)(4,1)}), s8[1048576]{0:T(1024)(128)(4,1)S(1)}, s32[]{:S(2)}) async-start(s8[5242880]{0:T(1024)(128)(4,1)} %bitcast.364), calls=%async_computation.4 | async-start | bytes 2097152
  112.1 26.0 %slice-start.1 = ((s8[5242880]{0:T(1024)(128)(4,1)}), s8[4194304]{0:T(1024)(128)(4,1)S(1)}, s32[]{:S(2)}) async-start(s8[5242880]{0:T(1024)(128)(4,1)} %bitcast.364), calls=%async_computation.5 | async-start | bytes 8388608
  165.0 13.7 copy-start
  165.0 13.7 copy-start.1
  165.0 13.6 copy-start.4
  165.0 13.6 copy-start.5
  166.2 10.6 collective-permute-start.5
  167.8 18.7 %copy-start.7 = (s32[3,3,8,8,4]{3,4,2,1,0:T(4,128)S(1)}, s32[3,3,8,8,4]{3,4,2,1,0:T(4,128)}, u32[]{:S(2)}) copy-start(s32[3,3,8,8,4]{3,4,2,1,0:T(4,128)} %param.11) | copy-start | bytes 27652
  167.8 10.8 collective-permute-start.4
  185.2 252.6 %collective-permute-start.6 = (f32[4,32,256,132]{2,1,3,0:T(8,128)}, f32[4,32,256,132]{2,1,3,0:T(8,128)}, u32[]{:S(2)}, u32[]{:S(2)}) collective-permute-start(f32[4,32,256,132]{2,1,3,0:T(8,128)} %pad_maximum_fusion.7), channel_id=1, source_target_pairs={{1,0},{2,1},{3,2},{4,3},{5,4},{6,5},{7,6},{9,8},{10,9},{11,10},{12... | collective-permute-start | bytes 51904520 | tf_op jit(solution)/shard_map/ppermute | solution.py:30
  286.2 0.6 copy-start.9
  341.2 94.0 %all-to-all-start = ((bf16[8,4,32768]{2,1,0:T(4,128)(2,1)}), bf16[8,4,32768]{2,1,0:T(4,128)(2,1)}, u32[]{:S(2)}, u32[]{:S(2)}) async-start(bf16[8,4,32768]{2,1,0:T(4,128)(2,1)} %scatter_fusion), calls=%async_computation | async-start | bytes 4194304 | tf_op jit(solution)/shard_map/all_to_all | solution.py:238
  531.1 425.1 %copy-start.31 = (s32[2,16]{1,0:T(2,128)S(1)}, s32[2,16]{1,0:T(2,128)}, u32[]{:S(2)}) copy-start(s32[2,16]{1,0:T(2,128)} %reshape_squeeze.31) | copy-start | bytes 388
  531.1 425.1 %copy-start.32 = (s32[2,16]{1,0:T(2,128)S(1)}, s32[2,16]{1,0:T(2,128)}, u32[]{:S(2)}) copy-start(s32[2,16]{1,0:T(2,128)} %reshape_squeeze.32) | copy-start | bytes 388
  531.1 425.1 %copy-start.34 = (s32[2,16]{1,0:T(2,128)S(1)}, s32[2,16]{1,0:T(2,128)}, u32[]{:S(2)}) copy-start(s32[2,16]{1,0:T(2,128)} %reshape_squeeze.30) | copy-start | bytes 388
  952.3 845.5 %all-to-all-start.1 = ((f32[8,1,144]{2,1,0:T(1,128)}), f32[8,1,144]{2,1,0:T(1,128)}, u32[]{:S(2)}, u32[]{:S(2)}) async-start(f32[8,1,144]{2,1,0:T(1,128)} %reshape.6259), calls=%async_computation.1 | async-start | bytes 16384 | tf_op jit(solution)/shard_map/all_to_all | solution.py:248
  956.2 417.3 %copy-start.29 = (s32[2,16]{1,0:T(2,128)S(1)}, s32[2,16]{1,0:T(2,128)}, u32[]{:S(2)}) copy-start(s32[2,16]{1,0:T(2,128)} %reshape_squeeze.34) | copy-start | bytes 388
  956.2 417.3 %copy-start.30 = (s32[2,16]{1,0:T(2,128)S(1)}, s32[2,16]{1,0:T(2,128)}, u32[]{:S(2)}) copy-start(s32[2,16]{1,0:T(2,128)} %reshape_squeeze.35) | copy-start | bytes 388
  956.3 417.3 %copy-start.33 = (s32[2,16]{1,0:T(2,128)S(1)}, s32[2,16]{1,0:T(2,128)}, u32[]{:S(2)}) copy-start(s32[2,16]{1,0:T(2,128)} %reshape_squeeze.33) | copy-start | bytes 388
  1373.5 0.6 copy-start.8
  1373.6 430.9 %copy-start.6 = (s32[32]{0:T(128)S(1)}, s32[32]{0:T(128)}, u32[]{:S(2)}) copy-start(s32[32]{0:T(128)} %get-tuple-element.603) | copy-start | bytes 388
  1373.6 461.0 %copy-start.20 = (f32[1,1,8,4]{3,2,1,0:T(8,128)S(1)}, f32[1,1,8,4]{3,2,1,0:T(8,128)}, u32[]{:S(2)}) copy-start(f32[1,1,8,4]{3,2,1,0:T(8,128)} %squeeze.533) | copy-start | bytes 388
  1373.6 461.0 %copy-start.21 = (f32[1,1,8,4]{3,2,1,0:T(8,128)S(1)}, f32[1,1,8,4]{3,2,1,0:T(8,128)}, u32[]{:S(2)}) copy-start(f32[1,1,8,4]{3,2,1,0:T(8,128)} %squeeze.513) | copy-start | bytes 388
  1373.6 461.0 %copy-start.22 = (f32[1,1,8,4]{3,2,1,0:T(8,128)S(1)}, f32[1,1,8,4]{3,2,1,0:T(8,128)}, u32[]{:S(2)}) copy-start(f32[1,1,8,4]{3,2,1,0:T(8,128)} %squeeze.530) | copy-start | bytes 388
  1373.6 461.0 %copy-start.23 = (f32[1,1,8,4]{3,2,1,0:T(8,128)S(1)}, f32[1,1,8,4]{3,2,1,0:T(8,128)}, u32[]{:S(2)}) copy-start(f32[1,1,8,4]{3,2,1,0:T(8,128)} %squeeze.509) | copy-start | bytes 388
  1373.6 461.0 %copy-start.24 = (f32[1,1,8,4]{3,2,1,0:T(8,128)S(1)}, f32[1,1,8,4]{3,2,1,0:T(8,128)}, u32[]{:S(2)}) copy-start(f32[1,1,8,4]{3,2,1,0:T(8,128)} %squeeze.526) | copy-start | bytes 388
  1373.6 461.0 %copy-start.25 = (f32[1,1,8,4]{3,2,1,0:T(8,128)S(1)}, f32[1,1,8,4]{3,2,1,0:T(8,128)}, u32[]{:S(2)}) copy-start(f32[1,1,8,4]{3,2,1,0:T(8,128)} %squeeze.504) | copy-start | bytes 388
  1373.6 461.0 %copy-start.26 = (f32[1,1,8,4]{3,2,1,0:T(8,128)S(1)}, f32[1,1,8,4]{3,2,1,0:T(8,128)}, u32[]{:S(2)}) copy-start(f32[1,1,8,4]{3,2,1,0:T(8,128)} %squeeze.512) | copy-start | bytes 388
  1373.6 461.0 %copy-start.27 = (f32[1,1,8,4]{3,2,1,0:T(8,128)S(1)}, f32[1,1,8,4]{3,2,1,0:T(8,128)}, u32[]{:S(2)}) copy-start(f32[1,1,8,4]{3,2,1,0:T(8,128)} %squeeze.508) | copy-start | bytes 388
  1373.7 461.0 %copy-start.28 = (f32[1,1,8,4]{3,2,1,0:T(8,128)S(1)}, f32[1,1,8,4]{3,2,1,0:T(8,128)}, u32[]{:S(2)}) copy-start(f32[1,1,8,4]{3,2,1,0:T(8,128)} %squeeze.503) | copy-start | bytes 388
  1794.3 41.3 %copy-start.10 = (f32[8,4]{1,0:T(8,128)S(1)}, f32[8,4]{1,0:T(8,128)}, u32[]{:S(2)}) copy-start(f32[8,4]{1,0:T(8,128)} %copy-done.9) | copy-start | bytes 388
  1794.3 41.4 %copy-start.11 = (f32[1,8,4]{2,1,0:T(8,128)S(1)}, f32[1,8,4]{2,1,0:T(8,128)}, u32[]{:S(2)}) copy-start(f32[1,8,4]{2,1,0:T(8,128)} %squeeze.611) | copy-start | bytes 388
  1794.3 41.4 %copy-start.12 = (f32[1,8,4]{2,1,0:T(8,128)S(1)}, f32[1,8,4]{2,1,0:T(8,128)}, u32[]{:S(2)}) copy-start(f32[1,8,4]{2,1,0:T(8,128)} %squeeze.591) | copy-start | bytes 388
  1794.3 41.4 %copy-start.13 = (f32[1,8,4]{2,1,0:T(8,128)S(1)}, f32[1,8,4]{2,1,0:T(8,128)}, u32[]{:S(2)}) copy-start(f32[1,8,4]{2,1,0:T(8,128)} %squeeze.608) | copy-start | bytes 388
  1794.4 41.4 %copy-start.14 = (f32[1,8,4]{2,1,0:T(8,128)S(1)}, f32[1,8,4]{2,1,0:T(8,128)}, u32[]{:S(2)}) copy-start(f32[1,8,4]{2,1,0:T(8,128)} %squeeze.587) | copy-start | bytes 388
  1794.4 41.4 %copy-start.15 = (f32[1,8,4]{2,1,0:T(8,128)S(1)}, f32[1,8,4]{2,1,0:T(8,128)}, u32[]{:S(2)}) copy-start(f32[1,8,4]{2,1,0:T(8,128)} %squeeze.604) | copy-start | bytes 388
  1794.4 41.4 %copy-start.16 = (f32[1,8,4]{2,1,0:T(8,128)S(1)}, f32[1,8,4]{2,1,0:T(8,128)}, u32[]{:S(2)}) copy-start(f32[1,8,4]{2,1,0:T(8,128)} %squeeze.582) | copy-start | bytes 388
  1794.4 41.4 %copy-start.17 = (f32[1,8,4]{2,1,0:T(8,128)S(1)}, f32[1,8,4]{2,1,0:T(8,128)}, u32[]{:S(2)}) copy-start(f32[1,8,4]{2,1,0:T(8,128)} %squeeze.590) | copy-start | bytes 388
  1794.4 41.4 %copy-start.18 = (f32[1,8,4]{2,1,0:T(8,128)S(1)}, f32[1,8,4]{2,1,0:T(8,128)}, u32[]{:S(2)}) copy-start(f32[1,8,4]{2,1,0:T(8,128)} %squeeze.586) | copy-start | bytes 388
  1794.4 41.4 %copy-start.19 = (f32[1,8,4]{2,1,0:T(8,128)S(1)}, f32[1,8,4]{2,1,0:T(8,128)}, u32[]{:S(2)}) copy-start(f32[1,8,4]{2,1,0:T(8,128)} %squeeze.581) | copy-start | bytes 388
  1797.7 10.7 all-to-all-start.2
  1808.4 10.7 all-to-all-start.3
where the time goes:
time: 1860 us; the launch traced here: 1840 us
  local copies, waits for them, and re-layouts  1050 us (56%)
  matrix products  348 us (19%)
  other arithmetic  311 us (17%)
  waiting for transfers between devices  64.1 us (3%)
  starting transfers between devices  58.7 us (3%)
    gather x288, local copies, waits for them, and re-layouts  677 us
    dot_general x6, matrix products, gram_from(): jnp.dot(window, window.T, precision=highest, preferred_element_type=jnp.f...  224 us
    reshape x6, local copies, waits for them, and re-layouts, one_whole(): window = lax.dynamic_slice(source, (0, z_first, y_first, x_first), (4, SU...  146 us
    dot_general x6, matrix products, gram_from(): jnp.dot(window, placed, precision=highest, preferred_element_type=jnp.flo...  123 us
    add x6, other arithmetic, tap_sum(): running + weights[tap_index] * lax.slice_in_dim(padded, tap_index, tap_in...  115 us
    reduce_sum x6, other arithmetic, gram_from(): field_total = jnp.sum(window, axis=1)  75.2 us
    while x1, local copies, waits for them, and re-layouts, slot_grams(): gram_set = lax.map(per_group, bundle)  68.8 us
    another operation x2, other arithmetic, body(): jnp.stack([tap_sum(def_gg, smooth, 0, planes), tap_sum(def_gg, slope, 0,...  52.8 us
  transfers between devices with their start and end apart: 11, of which 7 were waited for; matrix products, arithmetic and copies ran while one was open for 56% of the time, Pallas kernels for 0%

commit v1 on v0

--- a/solution.py
+++ b/solution.py
@@ -3,6 +3,8 @@
 import jax
 import jax.numpy as jnp
 from jax import lax
+from jax.experimental import pallas as pl
+from jax.experimental.pallas import tpu as pltpu
 from jax.sharding import PartitionSpec as P
 
 SUB = 32
@@ -144,44 +146,77 @@
     return (z_start, y_start, x_start)
 
 
-def gram_from(window, placed, inside):
-    highest = lax.Precision.HIGHEST
-    count = jnp.sum(inside) * (SUB * SUB)
-    ref_total = jnp.sum(placed)
-    field_total = jnp.sum(window, axis=1)
-    ref_square = jnp.dot(placed, placed, precision=highest, preferred_element_type=jnp.float32)
-    cross_ref = jnp.dot(window, placed, precision=highest, preferred_element_type=jnp.float32)
-    cross_field = jnp.dot(window, window.T, precision=highest, preferred_element_type=jnp.float32)
-    top_row = jnp.concatenate([jnp.stack([count, ref_total]), field_total])
-    second_row = jnp.concatenate([jnp.stack([ref_total, ref_square]), cross_ref])
-    lower_rows = jnp.concatenate([field_total[:, None], cross_ref[:, None], cross_field], axis=1)
-    return jnp.concatenate([top_row[None], second_row[None], lower_rows], axis=0)
-
-
-def slot_grams(source, arrived, z_start, y_start, x_start):
-    slabs, capacity, volume = arrived.shape
-    per_turn = 4
-    group_size = per_turn * capacity
-    slot_total = slabs * capacity
-
-    def one_whole(ref_block, z_first, y_first, x_first):
-        placed = ref_block.astype(jnp.float32)
-        window = lax.dynamic_slice(
-            source, (0, z_first, y_first, x_first), (4, SUB, SUB, SUB)
-        ).reshape(4, volume)
-        return gram_from(window, placed, jnp.ones((SUB,), jnp.float32))
-
-    def per_group(bundle):
-        return jax.vmap(one_whole)(bundle[0], bundle[1], bundle[2], bundle[3])
-
-    bundle = (
-        arrived.reshape(slot_total // group_size, group_size, volume),
-        z_start.reshape(-1, group_size),
-        y_start.reshape(-1, group_size),
-        x_start.reshape(-1, group_size),
-    )
-    gram_set = lax.map(per_group, bundle)
-    return gram_set.reshape(slabs, capacity, 6, 6)
+PAIRS = [(i, j) for i in range(4) for j in range(i, 4)]
+SUMS = 8 + len(PAIRS)
+
+
+def sums_kernel(x_first, z_tile, z_in, y_part, y_in, field_ref, ref_ref, out_ref):
+    step = pl.program_id(0)
+    z_off = z_in[step]
+    y_off = y_in[step]
+
+    def plane(ix, acc):
+        acc = list(acc)
+        placed = pltpu.roll(ref_ref[0, ix].astype(jnp.float32), y_off, 1)
+        for tile in range(SUB // 8):
+            f = [field_ref[i, ix, pl.ds(z_off + 8 * tile, 8), :] for i in range(4)]
+            r = placed[8 * tile : 8 * tile + 8]
+            for i in range(4):
+                acc[i] = acc[i] + f[i]
+                acc[4 + i] = acc[4 + i] + f[i] * r
+            for n, (i, j) in enumerate(PAIRS):
+                acc[8 + n] = acc[8 + n] + f[i] * f[j]
+        return tuple(acc)
+
+    zero = jnp.zeros((8, 128), jnp.float32)
+    acc = lax.fori_loop(0, SUB, plane, (zero,) * SUMS)
+    lane = lax.broadcasted_iota(jnp.int32, (1, 128), 1)
+    inside = (lane >= y_off) & (lane < y_off + SUB)
+    for n in range(SUMS):
+        total = jnp.sum(acc[n], axis=0, keepdims=True)
+        out_ref[0, n : n + 1, :] = jnp.where(inside, total, 0.0)
+
+
+def slot_sums(parts, arrived, z_start, y_start, x_start):
+    slots = arrived.shape[0]
+    steps = slots * ITERS
+    z_all, y_all, x_all = [v.reshape(ITERS, slots).T.reshape(steps) for v in (z_start, y_start, x_start)]
+    z_tile = jnp.minimum(z_all // 8, 3)
+    y_part = jnp.where(y_all <= 96, 0, jnp.where(y_all >= 128, 2, 1))
+    scalars = (x_all, z_tile, z_all - 8 * z_tile, y_part, y_all - 64 * y_part)
+    element = pl.Element
+    spec = pltpu.PrefetchScalarGridSpec(
+        num_scalar_prefetch=5,
+        grid=(steps,),
+        in_specs=[
+            pl.BlockSpec(
+                (element(4), element(SUB), element(SUB + 8), element(128)),
+                lambda s, x, zt, zi, yp, yi: (0, x[s], zt[s] * 8, yp[s] * 128),
+            ),
+            pl.BlockSpec((1, SUB, SUB, 128), lambda s, *_: (s // ITERS, 0, 0, 0)),
+        ],
+        out_specs=pl.BlockSpec((1, SUMS, 128), lambda s, *_: (s, 0, 0)),
+    )
+    sums = pl.pallas_call(
+        sums_kernel,
+        grid_spec=spec,
+        out_shape=jax.ShapeDtypeStruct((steps, SUMS, 128), jnp.float32),
+        compiler_params=pltpu.CompilerParams(vmem_limit_bytes=32 * 1024 * 1024),
+    )(*scalars, parts, arrived)
+    return jnp.sum(sums, axis=2).reshape(slots, ITERS * SUMS)
+
+
+def gram_of(sums, ref_total, ref_square, volume):
+    count = jnp.full(ref_total.shape, volume, jnp.float32)
+    pair = {}
+    for n, (i, j) in enumerate(PAIRS):
+        pair[i, j] = pair[j, i] = sums[:, 8 + n]
+    rows = [
+        [count, ref_total] + [sums[:, i] for i in range(4)],
+        [ref_total, ref_square] + [sums[:, 4 + i] for i in range(4)],
+    ]
+    rows += [[sums[:, i], sums[:, 4 + i]] + [pair[i, j] for j in range(4)] for i in range(4)]
+    return jnp.stack([jnp.stack(row, axis=-1) for row in rows], axis=-2)
 
 
 def body(ref_scan, def_scan, offsets):
@@ -215,7 +250,7 @@
     volume = SUB * SUB * SUB
     blocks = (
         smoothed.reshape(SUB, sub_y, SUB, sub_x, SUB)
-        .transpose(1, 3, 0, 2, 4)
+        .transpose(1, 3, 4, 0, 2)
         .reshape(subsets, volume)
     )
     ref_mean = jnp.mean(blocks, axis=1)
@@ -237,16 +272,26 @@
     outgoing = jnp.zeros((slabs, capacity, volume), jnp.bfloat16).at[my_owner, my_rank].set(normed)
     arrived = lax.all_to_all(outgoing, "slab", split_axis=0, concat_axis=0, tiled=True)
     plan_own = slot_plan(route_table, owners, slot_rank, me_slab, capacity, sub_x)
-    beyond = from_behind(fields_wide, "slab", -1)
-    tall = jnp.concatenate([fields_wide, beyond], axis=1)
+    turned = fields_wide.transpose(0, 3, 1, 2)
+    half = rows_all // 4
+    beyond = from_behind(turned, "slab", -1)
+    tall = jnp.concatenate([turned, beyond], axis=2)
+    parts = jnp.concatenate(
+        [tall[..., :128], tall[..., half : half + 128], tall[..., 128:]], axis=3
+    )
+    cubes = arrived.reshape(slabs * capacity, SUB, SUB, SUB)
+    cubes = jnp.concatenate([cubes] * 4, axis=3)
+    ref_total = jnp.sum(normed.astype(jnp.float32), axis=1)
+    ref_square = jnp.sum(normed.astype(jnp.float32) ** 2, axis=1)
+    sums = slot_sums(parts, cubes, *plan_own)
+    returned = lax.all_to_all(
+        sums.reshape(slabs, capacity, ITERS * SUMS), "slab", split_axis=0, concat_axis=0, tiled=True
+    )
+    mine = returned[my_owner, my_rank].reshape(subsets, ITERS, SUMS)
     my_table = lax.dynamic_index_in_dim(route_table, me_slab, 2, keepdims=False).astype(jnp.float32)
     current = [jnp.zeros((subsets,), jnp.float32) for index_a in range(3)]
     for turn_index in range(ITERS):
-        slot_sums = slot_grams(
-            tall, arrived, plan_own[0][turn_index], plan_own[1][turn_index], plan_own[2][turn_index]
-        )
-        returned = lax.all_to_all(slot_sums, "slab", split_axis=0, concat_axis=0, tiled=True)
-        my_grams = returned[my_owner, my_rank]
+        my_grams = gram_of(mine[:, turn_index], ref_total, ref_square, float(volume))
         newest, moment_set = gauss_newton(my_grams, current)
         if turn_index + 1 < ITERS:
             current = [

time: 1860 us -> 840 us (0.45)
  local copies, waits for them, and re-layouts: 1050 us -> 129 us
  matrix products: 348 us -> 0 us
  Pallas kernels: 0 us -> 245 us
  waiting for transfers between devices: 64.1 us -> 88.6 us
    gather x291 -> x2, local copies, waits for them, and re-layouts: 679 us -> 0.76 us  [body(): mine = returned[my_owner, my_rank].reshape(subsets, ITERS, SUMS)]
    dot_general x12 -> x0, matrix products: 348 us -> none  [the longest x6 224 us: gram_from(): jnp.dot(window, window.T, precision=highest, preferred_element_type=jnp.f...]
    pallas_call x0 -> x1, Pallas kernels: none -> 245 us  [slot_sums(): pl.pallas_call(sums_kernel, grid_spec=spec, out_shape=jax.ShapeDtypeStruc...]
    reshape x16 -> x8, local copies, waits for them, and re-layouts: 191 us -> 44.1 us  [the longest x2 25.2 us: body(): smoothed.reshape(SUB, sub_y, SUB, sub_x, SUB).transpose(1, 3, 4, 0, 2)]
    while x1 -> x0, local copies, waits for them, and re-layouts: 68.8 us -> none  [slot_grams(): gram_set = lax.map(per_group, bundle)]
    reduce_sum x13 -> x3, other arithmetic: 78.1 us -> 11.2 us  [the longest x1 10.6 us: body(): ref_square = jnp.sum(normed.astype(jnp.float32) ** 2, axis=1)]
    concatenate x19 -> x3, other arithmetic: 25.7 us -> 89.4 us  [the longest x1 39.3 us: body(): jnp.concatenate([tall[..., :128], tall[..., half:half + 128], tall[..., 1...]
    add x6, other arithmetic: 115 us -> 134 us  [tap_sum(): running + weights[tap_index] * lax.slice_in_dim(padded, tap_index, tap_in...]
  transfers between devices with their start and end apart: 11 -> 9, of which waited for: 7 -> 6; matrix products, arithmetic and copies ran while one was open for 56% -> 24% of each run, Pallas kernels for 0% -> 0%
where the time goes in v1:
time: 840 us; the launch traced here: 830 us
  other arithmetic  324 us (39%)
  Pallas kernels  245 us (29%)
  local copies, waits for them, and re-layouts  129 us (15%)
  waiting for transfers between devices  88.6 us (11%)
  starting transfers between devices  41.3 us (5%)
    pallas_call x1, Pallas kernels, slot_sums(): pl.pallas_call(sums_kernel, grid_spec=spec, out_shape=jax.ShapeDtypeStruc...  245 us
    add x6, other arithmetic, tap_sum(): running + weights[tap_index] * lax.slice_in_dim(padded, tap_index, tap_in...  134 us
    all_to_all x1, waiting for transfers between devices, body(): lax.all_to_all(outgoing, 'slab', split_axis=0, concat_axis=0, tiled=True)  67.3 us
    scatter x1, local copies, waits for them, and re-layouts, body(): jnp.zeros((slabs, capacity, volume), jnp.bfloat16).at[my_owner, my_rank]  41.9 us
    concatenate x1, other arithmetic, body(): jnp.concatenate([tall[..., :128], tall[..., half:half + 128], tall[..., 1...  39.3 us
    another operation x3, other arithmetic, body(): jnp.stack([tap_sum(def_gg, smooth, 0, planes), tap_sum(def_gg, slope, 0,...  37.2 us
    concatenate x1, other arithmetic, body(): tall = jnp.concatenate([turned, beyond], axis=2)  29.1 us
    reshape x2, local copies, waits for them, and re-layouts, body(): smoothed.reshape(SUB, sub_y, SUB, sub_x, SUB).transpose(1, 3, 4, 0, 2)  25.2 us
  transfers between devices with their start and end apart: 9, of which 6 were waited for; matrix products, arithmetic and copies ran while one was open for 24% of the time, Pallas kernels for 0%

profile of v1, /device:TPU:0, one launch (start us, length us, event | category | flops | bytes accessed | tf_op | source)
XLA Modules:
  0.0 830.1 jit_solution(10178176558045133250)
XLA Ops:
  0.6 5.5 copy.168
  6.1 5.5 copy.169
  11.6 1.3 pad_maximum_fusion.11
  12.9 5.1 collective-permute-start
  18.0 1.3 collective-permute-start.1
  19.3 4.2 collective-permute-done
  23.5 7.6 collective-permute-done.1
  31.1 0.4 pad_maximum_fusion.5
  31.5 0.3 copy-done.7
  31.8 1.3 collective-permute-start.2
  33.2 1.3 collective-permute-start.3
  34.5 1.0 copy.156
  35.6 0.7 broadcast_compare_fusion
  36.3 3.4 collective-permute-done.3
  39.7 11.0 %pad_maximum_fusion = f32[2,40,256,136]{2,1,3,0:T(8,128)} fusion(f32[2,4,256,136]{2,1,3,0:T(4,128)} %collective-permute-done.3, f32[2,32,256,4]{2,1,3,0:T(8,128)} %copy-done.7, f32[1,32,256,128]{2,1,3,0:T(8,128)} %bitcast.277, f32[1,32,256,128]{2,1,3,0:T(8,128)} %bitcast.274, f32[2,32,256,4]{2,1,3,0:T(8,128)} %copy-done.6, ...), kind=kLoop, calls=%fused_computation.42 | loop fusion | flops 13926400 | bytes 22282240 | tf_op jit(solution)/shard_map/concatenate | solution.py:25
  50.7 7.3 slice_bitcast_fusion.1
  58.0 8.4 %multiply_add_fusion.3 = (f32[40,256,128]{1,0,2:T(8,128)}, f32[40,256,128]{1,0,2:T(8,128)}) fusion(f32[40,256,136]{1,0,2:T(8,128)S(1)} %get-tuple-element.130), kind=kLoop, calls=%fused_computation.98 | loop fusion | flops 44564480 | bytes 57671680 | tf_op jit(solution)/shard_map/add | solution.py:48
  66.4 45.9 %multiply_add_fusion.2 = (f32[40,256,128]{1,0,2:T(8,128)}, f32[40,256,128]{1,0,2:T(8,128)}) fusion(f32[40,256,128]{1,0,2:T(8,128)} %get-tuple-element.136), kind=kLoop, calls=%fused_computation.97 | loop fusion | flops 44564480 | bytes 15728640 | tf_op jit(solution)/shard_map/add | solution.py:48
  112.4 25.3 %add_bitcast_fusion.1 = (f32[1,32,256,128]{2,1,3,0:T(8,128)}, f32[1,32,256,128]{2,1,3,0:T(8,128)}) fusion(f32[40,256,128]{1,0,2:T(8,128)} %get-tuple-element.140), kind=kLoop, calls=%fused_computation.154 | loop fusion | flops 35651584 | bytes 46137344 | tf_op jit(solution)/shard_map/stack | solution.py:238
  137.7 6.1 fusion.62
  143.7 27.3 %fusion.12 = f32[40,256,128]{1,0,2:T(8,128)S(1)} fusion(f32[40,256,128]{1,0,2:T(8,128)} %get-tuple-element.137), kind=kLoop, calls=%fused_computation.54 | loop fusion | flops 22282240 | bytes 10485760 | tf_op jit(solution)/shard_map/add | solution.py:48
  171.1 5.9 fusion.53
  176.9 1.1 pad_maximum_fusion.9
  178.0 3.4 collective-permute-start.4
  181.5 1.3 collective-permute-start.5
  182.8 0.3 convert_reduce_fusion.2
  183.1 0.5 fusion.251
  183.6 1.7 collective-permute-done.4
  185.3 4.4 collective-permute-done.5
  189.7 11.8 %maximum_bitcast_fusion = f32[4,132,32,256]{3,2,1,0:T(8,128)} fusion(f32[4,32,256,2]{2,1,3,0:T(8,128)S(1)} %collective-permute-done.5, f32[1,32,256,128]{2,1,3,0:T(8,128)} %fusion.53, f32[1,32,256,128]{2,1,3,0:T(8,128)} %fusion.62, f32[1,32,256,128]{2,1,3,0:T(8,128)} %get-tuple-element.139, f32[1,32,256,128]{2,1,3,0:T(8,128)} %get-tuple-element.138, ...), kind=kLoop, calls=%fused_computation.13 | loop fusion | flops 21626880 | bytes 34603008 | tf_op jit(solution)/shard_map/transpose | solution.py:275
  201.5 1.3 collective-permute-start.6
  202.8 19.6 %fusion.36 = f32[40,256,128]{1,0,2:T(8,128)} fusion(f32[40,256,136]{1,0,2:T(8,128)} %get-tuple-element.131), kind=kLoop, calls=%fused_computation.79 | loop fusion | flops 22282240 | bytes 52428800 | tf_op jit(solution)/shard_map/add | solution.py:48
  222.4 27.3 %fusion.28 = f32[40,256,128]{1,0,2:T(8,128)S(1)} fusion(f32[40,256,128]{1,0,2:T(8,128)} %fusion.36), kind=kLoop, calls=%fused_computation.70 | loop fusion | flops 22282240 | bytes 10485760 | tf_op jit(solution)/shard_map/add | solution.py:48
  249.7 5.9 fusion.44
  255.6 10.9 %reshape.5646 = f32[32,8,32,4,32]{2,1,0,4,3:T(8,128)} reshape(f32[32,256,128]{1,0,2:T(8,128)} %fusion.44) | data formatting | bytes 8388608 | tf_op jit(solution)/shard_map/reshape | solution.py:252
  266.5 14.3 %copy.196 = f32[32,8,32,4,32]{2,0,4,3,1:T(8,128)} copy(f32[32,8,32,4,32]{2,1,0,4,3:T(8,128)} %reshape.5646) | data formatting | bytes 8388608 | tf_op jit(solution)/shard_map/reshape | solution.py:252
  280.9 9.4 %fusion.252 = f32[8,4]{1,0:T(8,128)S(1)} fusion(f32[32,8,32,4,32]{2,1,0,4,3:T(8,128)} %reshape.5646), kind=kLoop, calls=%fused_computation.635 | loop fusion | flops 1048544 | bytes 4194432 | tf_op jit(solution)/shard_map/reduce_sum | solution.py:256
  290.3 10.1 %multiply_reduce_fusion = f32[8,4]{1,0:T(8,128)S(1)} fusion(f32[8,4]{1,0:T(8,128)S(1)} %broadcast_multiply_fusion, f32[32,8,32,4,32]{2,1,0,4,3:T(8,128)} %reshape.5646), kind=kLoop, calls=%fused_computation.17 | loop fusion | flops 3145696 | bytes 4194560 | tf_op jit(solution)/shard_map/reduce_sum | solution.py:259
  300.5 11.6 %reshape.5647 = f32[32,32768]{1,0:T(8,128)} reshape(f32[8,4,32,32,32]{4,3,2,1,0:T(8,128)} %bitcast.272) | data formatting | bytes 8388608 | tf_op jit(solution)/shard_map/reshape | solution.py:254
  312.1 2.6 divide_convert_fusion.1
  314.8 1.9 broadcast_in_dim.30
  316.7 41.9 %scatter_fusion = bf16[8,4,32768]{2,1,0:T(4,128)(2,1)} fusion(bf16[8,4,32768]{2,1,0:T(4,128)(2,1)} %broadcast_in_dim.30, s32[32]{0:T(128)S(1)} %get-tuple-element.205, bf16[32,32768]{1,0:T(8,128)(2,1)S(1)} %divide_convert_fusion.1), kind=kCustom, calls=%fused_computation.1 | custom fusion | bytes 6291712 | tf_op jit(solution)/shard_map/scatter | solution.py:272
  358.6 22.6 %all-to-all-start = ((bf16[8,4,32768]{2,1,0:T(4,128)(2,1)}), bf16[8,4,32768]{2,1,0:T(4,128)(2,1)S(1)}, u32[]{:S(2)}, u32[]{:S(2)}) async-start(bf16[8,4,32768]{2,1,0:T(4,128)(2,1)} %scatter_fusion), calls=%async_computation | async-start | bytes 4194304 | tf_op jit(solution)/shard_map/all_to_all | solution.py:273
  381.2 0.7 multiply_reduce_fusion.1
  382.5 0.3 select_reduce_fusion
  384.1 0.2 convert_reduce_fusion.1
  385.8 67.3 %all-to-all-done = bf16[8,4,32768]{2,1,0:T(4,128)(2,1)S(1)} async-done(((bf16[8,4,32768]{2,1,0:T(4,128)(2,1)}), bf16[8,4,32768]{2,1,0:T(4,128)(2,1)S(1)}, u32[]{:S(2)}, u32[]{:S(2)}) %all-to-all-start) | async-done | bytes 2097184 | tf_op jit(solution)/shard_map/all_to_all | solution.py:273
  453.1 6.9 reshape.5648
  459.9 21.0 %pad_maximum_fusion.1.ref_ref = bf16[32,32,32,128]{3,2,1,0:T(8,128)(2,1)} fusion(bf16[32,32,32,32]{3,2,1,0:T(8,128)(2,1)} %reshape.5648), kind=kLoop, calls=%fused_computation.43 | loop fusion | flops 33554432 | bytes 10485760 | tf_op jit(solution)/shard_map/concatenate | solution.py:283
  480.9 29.1 %fusion.2 = (f32[4,132,64,128]{3,2,1,0:T(8,128)}, f32[4,132,64,128]{3,2,1,0:T(8,128)}) fusion(f32[4,132,32,256]{3,2,1,0:T(8,128)} %maximum_bitcast_fusion, f32[4,132,32,256]{3,2,1,0:T(8,128)} %collective-permute-done.6), kind=kLoop, calls=%fused_computation.12 | loop fusion | flops 8650752 | bytes 69206016 | tf_op jit(solution)/shard_map/concatenate | solution.py:278
  510.0 39.3 %fusion.field_ref = f32[4,132,64,384]{3,2,1,0:T(8,128)} fusion(f32[4,132,32,256]{3,2,1,0:T(8,128)} %collective-permute-done.6, f32[4,132,32,256]{3,2,1,0:T(8,128)} %maximum_bitcast_fusion, f32[4,132,64,128]{3,2,1,0:T(8,128)} %get-tuple-element.127, f32[4,132,64,128]{3,2,1,0:T(8,128)} %get-tuple-element.126), kind=kLoop, calls=%fused_computation.3 | loop fusion | flops 77856768 | bytes 121110528 | tf_op jit(solution)/shard_map/concatenate | solution.py:279
  549.3 3.4 copy-done
  552.7 245.4 %shard_map.58 = f32[96,18,128]{2,1,0:T(8,128)S(1)} custom-call(s32[96]{0:T(128)S(1)} %reshape.5643.x_first, s32[96]{0:T(128)S(1)} %get-tuple-element.123.z_tile, s32[96]{0:T(128)S(1)} %get-tuple-element.122.z_in, s32[96]{0:T(128)S(1)} %get-tuple-element.291.y_part, s32[96]{0:T(128)S(1)} %get-tuple-element.290.y_in, f32[4,132,64,384]{3,2,1,0:T(8,128)} %fusion.field_ref, ...), custom_call_target="tpu_custom_call" | custom-call | tf_op jit(solution)/shard_map/pallas_call | solution.py:200
  798.1 0.4 reduce_sum.97
  798.6 0.7 reshape.6271
  799.2 3.6 all-to-all-start.1
  802.9 10.6 %fusion.3 = (f32[8,4]{1,0:T(8,128)S(1)}, f32[8,4]{1,0:T(8,128)S(1)}) fusion(f32[8,4]{1,0:T(8,128)S(1)} %add_sqrt_fusion, f32[8,4]{1,0:T(8,128)S(1)} %broadcast_multiply_fusion, f32[32,8,32,4,32]{2,1,0,4,3:T(8,128)} %reshape.5646), kind=kLoop, calls=%fused_computation.14 | loop fusion | flops 7339968 | bytes 4194816 | tf_op jit(solution)/shard_map/reduce_sum | solution.py:285
  813.6 0.5 broadcast.1522
  814.1 0.7 reduce.460
  814.9 0.7 gather_fusion
  816.2 0.7 copy.183
  822.7 0.7 copy.182
  828.7 0.1 divide_subtract_fusion.2
  828.9 0.7 copy.181
  (265 shorter events, 15.4 us)
Async XLA Ops:
  11.6 19.5 %copy-start.2 = (f32[32,256,128]{1,0,2:T(8,128)S(1)}, f32[32,256,128]{1,0,2:T(8,128)}, u32[]{:S(2)}) copy-start(f32[32,256,128]{1,0,2:T(8,128)} %copy.168) | copy-start | bytes 12582916
  11.6 19.5 %copy-start.3 = (f32[32,256,128]{1,0,2:T(8,128)S(1)}, f32[32,256,128]{1,0,2:T(8,128)}, u32[]{:S(2)}) copy-start(f32[32,256,128]{1,0,2:T(8,128)} %copy.169) | copy-start | bytes 12582916
  12.9 10.7 %collective-permute-start = (f32[2,32,256,4]{2,1,3,0:T(8,128)S(1)}, f32[2,32,256,4]{2,1,3,0:T(8,128)S(1)}, u32[]{:S(2)}, u32[]{:S(2)}) collective-permute-start(f32[2,32,256,4]{2,1,3,0:T(8,128)S(1)} %get-tuple-element.134), channel_id=1, source_target_pairs={{0,8},{8,16},{16,24},{1,9},{9,17},{17,25},{2,10},{10,18},{18,26},{... | collective-permute-start | bytes 786440 | tf_op jit(solution)/shard_map/ppermute | solution.py:23
  18.0 13.1 %collective-permute-start.1 = (f32[2,32,256,4]{2,1,3,0:T(8,128)S(1)}, f32[2,32,256,4]{2,1,3,0:T(8,128)S(1)}, u32[]{:S(2)}, u32[]{:S(2)}) collective-permute-start(f32[2,32,256,4]{2,1,3,0:T(8,128)S(1)} %get-tuple-element.135), channel_id=1, source_target_pairs={{8,0},{16,8},{24,16},{9,1},{17,9},{25,17},{10,2},{18,10},{26,18},{... | collective-permute-start | bytes 786440 | tf_op jit(solution)/shard_map/ppermute | solution.py:24
  23.5 8.0 copy-start.6
  31.1 0.7 copy-start.7
  31.8 4.5 collective-permute-start.2
  33.2 6.5 collective-permute-start.3
  35.5 15.2 %copy-start.4 = (s32[3,3,8,8,4]{2,4,3,1,0:T(4,128)}, s32[3,3,8,8,4]{2,4,3,1,0:T(4,128)S(1)}, u32[]{:S(2)}) copy-start(s32[3,3,8,8,4]{2,4,3,1,0:T(4,128)S(1)} %copy.156) | copy-start | bytes 27652
  35.6 15.1 %copy-start.9 = (s32[3,3,8,32]{3,2,1,0:T(8,128)}, s32[3,3,8,32]{3,2,1,0:T(8,128)S(1)}, u32[]{:S(2)}) copy-start(s32[3,3,8,32]{3,2,1,0:T(8,128)S(1)} %copy.157) | copy-start | bytes 27652
  35.6 0.7 copy-start.12
  112.4 25.3 %copy-start.1 = (f32[40,256,128]{1,0,2:T(8,128)S(1)}, f32[40,256,128]{1,0,2:T(8,128)}, u32[]{:S(2)}) copy-start(f32[40,256,128]{1,0,2:T(8,128)} %get-tuple-element.141) | copy-start | bytes 15728644
  178.0 7.3 collective-permute-start.4
  181.5 8.3 collective-permute-start.5
  201.5 279.4 %collective-permute-start.6 = (f32[4,132,32,256]{3,2,1,0:T(8,128)}, f32[4,132,32,256]{3,2,1,0:T(8,128)}, u32[]{:S(2)}, u32[]{:S(2)}) collective-permute-start(f32[4,132,32,256]{3,2,1,0:T(8,128)} %maximum_bitcast_fusion), channel_id=1, source_target_pairs={{1,0},{2,1},{3,2},{4,3},{5,4},{6,5},{7,6},{9,8},{10,9},{11,10},{12... | collective-permute-start | bytes 51904520 | tf_op jit(solution)/shard_map/ppermute | solution.py:32
  316.7 64.5 %copy-start.11 = (pred[8,32]{1,0:T(8,128)(4,1)S(1)}, pred[8,32]{1,0:T(8,128)(4,1)}, u32[]{:S(2)}) copy-start(pred[8,32]{1,0:T(8,128)(4,1)} %get-tuple-element.124) | copy-start | bytes 772
  316.7 64.5 %copy-start.10 = (s32[3,3,8,32]{3,2,1,0:T(8,128)S(1)}, s32[3,3,8,32]{3,2,1,0:T(8,128)}, u32[]{:S(2)}) copy-start(s32[3,3,8,32]{3,2,1,0:T(8,128)} %copy-done.9) | copy-start | bytes 27652
  316.7 66.6 %copy-start.13 = (s32[8]{0:T(128)S(1)}, s32[8]{0:T(128)}, u32[]{:S(2)}) copy-start(s32[8]{0:T(128)} %copy-done.12) | copy-start | bytes 100
  316.7 67.4 %copy-start.5 = (s32[3,3,8,8,4]{2,4,3,1,0:T(4,128)S(1)}, s32[3,3,8,8,4]{2,4,3,1,0:T(4,128)}, u32[]{:S(2)}) copy-start(s32[3,3,8,8,4]{2,4,3,1,0:T(4,128)} %copy-done.4) | copy-start | bytes 27652
  358.6 94.5 %all-to-all-start = ((bf16[8,4,32768]{2,1,0:T(4,128)(2,1)}), bf16[8,4,32768]{2,1,0:T(4,128)(2,1)S(1)}, u32[]{:S(2)}, u32[]{:S(2)}) async-start(bf16[8,4,32768]{2,1,0:T(4,128)(2,1)} %scatter_fusion), calls=%async_computation | async-start | bytes 4194304 | tf_op jit(solution)/shard_map/all_to_all | solution.py:273
  549.3 3.4 copy-start
  799.2 14.4 %all-to-all-start.1 = ((f32[8,1,216]{2,1,0:T(1,128)}), f32[8,1,216]{2,1,0:T(1,128)S(1)}, u32[]{:S(2)}, u32[]{:S(2)}) async-start(f32[8,1,216]{2,1,0:T(1,128)} %reshape.6271), calls=%async_computation.1 | async-start | bytes 16384 | tf_op jit(solution)/shard_map/all_to_all | solution.py:287
  802.9 12.0 %copy-start.8 = (s32[32]{0:T(128)S(1)}, s32[32]{0:T(128)}, u32[]{:S(2)}) copy-start(s32[32]{0:T(128)} %get-tuple-element.204) | copy-start | bytes 388

commit v2 on v1

--- a/solution.py
+++ b/solution.py
@@ -2,6 +2,7 @@
 
 import jax
 import jax.numpy as jnp
+import numpy as np
 from jax import lax
 from jax.experimental import pallas as pl
 from jax.experimental.pallas import tpu as pltpu
@@ -51,10 +52,17 @@
     return running
 
 
-def zero_pad(values, which_axis):
-    widths = [(0, 0)] * values.ndim
-    widths[which_axis] = (RIM, RIM)
-    return jnp.pad(values, widths)
+def rows_filtered(values, weights):
+    rows = values.shape[1]
+    band = jnp.asarray(
+        sum(w * np.eye(rows, k=RIM - t) for t, w in enumerate(weights)), jnp.float32
+    )
+    planes, _, cols = values.shape
+    lines = values.transpose(2, 0, 1).reshape(cols * planes, rows)
+    done = jnp.dot(
+        lines, band, precision=lax.Precision.HIGHEST, preferred_element_type=jnp.float32
+    )
+    return done.reshape(cols, planes, rows).transpose(1, 2, 0)
 
 
 def solve_three(k_mat, rhs_vec):
@@ -159,7 +167,7 @@
         acc = list(acc)
         placed = pltpu.roll(ref_ref[0, ix].astype(jnp.float32), y_off, 1)
         for tile in range(SUB // 8):
-            f = [field_ref[i, ix, pl.ds(z_off + 8 * tile, 8), :] for i in range(4)]
+            f = [field_ref[0, i, ix, pl.ds(z_off + 8 * tile, 8), :] for i in range(4)]
             r = placed[8 * tile : 8 * tile + 8]
             for i in range(4):
                 acc[i] = acc[i] + f[i]
@@ -169,7 +177,7 @@
         return tuple(acc)
 
     zero = jnp.zeros((8, 128), jnp.float32)
-    acc = lax.fori_loop(0, SUB, plane, (zero,) * SUMS)
+    acc = lax.fori_loop(0, SUB, plane, (zero,) * SUMS, unroll=4)
     lane = lax.broadcasted_iota(jnp.int32, (1, 128), 1)
     inside = (lane >= y_off) & (lane < y_off + SUB)
     for n in range(SUMS):
@@ -190,8 +198,8 @@
         grid=(steps,),
         in_specs=[
             pl.BlockSpec(
-                (element(4), element(SUB), element(SUB + 8), element(128)),
-                lambda s, x, zt, zi, yp, yi: (0, x[s], zt[s] * 8, yp[s] * 128),
+                (element(1), element(4), element(SUB), element(SUB + 8), element(128)),
+                lambda s, x, zt, zi, yp, yi: (yp[s], 0, x[s], zt[s] * 8, 0),
             ),
             pl.BlockSpec((1, SUB, SUB, 128), lambda s, *_: (s // ITERS, 0, 0, 0)),
         ],
@@ -229,11 +237,10 @@
     ref_x = tap_sum(grown[0], smooth, 2, cols_dev)
     def_gx = tap_sum(grown[1], smooth, 2, cols_dev)
     def_dx = tap_sum(grown[1], slope, 2, cols_dev)
-    ref_xy = tap_sum(zero_pad(ref_x, 1), smooth, 1, rows_all)
-    gx_pad = zero_pad(def_gx, 1)
-    def_gg = tap_sum(gx_pad, smooth, 1, rows_all)
-    def_dg = tap_sum(gx_pad, slope, 1, rows_all)
-    def_gd = tap_sum(zero_pad(def_dx, 1), smooth, 1, rows_all)
+    ref_xy = rows_filtered(ref_x, smooth)
+    def_gg = rows_filtered(def_gx, smooth)
+    def_dg = rows_filtered(def_gx, slope)
+    def_gd = rows_filtered(def_dx, smooth)
     smoothed = tap_sum(ref_xy, smooth, 0, planes)
     fields = jnp.stack(
         [
@@ -269,16 +276,19 @@
     capacity = max(2, (subsets + slabs - 1) // slabs)
     my_owner = lax.dynamic_index_in_dim(owners, me_slab, 0, keepdims=False)
     my_rank = lax.dynamic_index_in_dim(slot_rank, me_slab, 0, keepdims=False)
-    outgoing = jnp.zeros((slabs, capacity, volume), jnp.bfloat16).at[my_owner, my_rank].set(normed)
+    my_slot = my_owner * capacity + my_rank
+    chosen = (
+        jnp.arange(slabs * capacity, dtype=jnp.int32)[:, None] == my_slot[None, :]
+    ).astype(jnp.bfloat16)
+    outgoing = jnp.dot(chosen, normed, preferred_element_type=jnp.float32)
+    outgoing = outgoing.astype(jnp.bfloat16).reshape(slabs, capacity, volume)
     arrived = lax.all_to_all(outgoing, "slab", split_axis=0, concat_axis=0, tiled=True)
     plan_own = slot_plan(route_table, owners, slot_rank, me_slab, capacity, sub_x)
     turned = fields_wide.transpose(0, 3, 1, 2)
     half = rows_all // 4
     beyond = from_behind(turned, "slab", -1)
     tall = jnp.concatenate([turned, beyond], axis=2)
-    parts = jnp.concatenate(
-        [tall[..., :128], tall[..., half : half + 128], tall[..., 128:]], axis=3
-    )
+    parts = jnp.stack([tall[..., :128], tall[..., half : half + 128], tall[..., 128:]])
     cubes = arrived.reshape(slabs * capacity, SUB, SUB, SUB)
     cubes = jnp.concatenate([cubes] * 4, axis=3)
     ref_total = jnp.sum(normed.astype(jnp.float32), axis=1)

time: 840 us -> 677 us (0.81)
  Pallas kernels: 245 us -> 127 us
  other arithmetic: 324 us -> 218 us
  matrix products: 0 us -> 55.9 us
  waiting for transfers between devices: 88.6 us -> 143 us
  local copies, waits for them, and re-layouts: 129 us -> 85.3 us
    pallas_call x1, Pallas kernels: 245 us -> 127 us  [slot_sums(): pl.pallas_call(sums_kernel, grid_spec=spec, out_shape=jax.ShapeDtypeStruc...]
    add x6 -> x2, other arithmetic: 134 us -> 39 us  [tap_sum(): running + weights[tap_index] * lax.slice_in_dim(padded, tap_index, tap_in...]
    another operation x0 -> x2, other arithmetic: none -> 75.2 us  [body(): jnp.stack([tall[..., :128], tall[..., half:half + 128], tall[..., 128:]])]
    concatenate x3 -> x1, other arithmetic: 69 us -> 0.07 us  [body(): mine = returned[my_owner, my_rank].reshape(subsets, ITERS, SUMS)]
    dot_general x0 -> x5, matrix products: none -> 55.9 us  [the longest x4 53 us: rows_filtered(): jnp.dot(lines, band, precision=lax.Precision.HIGHEST, preferred_element_t...]
    all_to_all x1, waiting for transfers between devices: 67.3 us -> 120 us  [body(): lax.all_to_all(outgoing, 'slab', split_axis=0, concat_axis=0, tiled=True)]
    scatter x1 -> x0, local copies, waits for them, and re-layouts: 41.9 us -> none  [body(): jnp.zeros((slabs, capacity, volume), jnp.bfloat16).at[my_owner, my_rank]]
    unnamed x36 -> x32, local copies, waits for them, and re-layouts: 18.5 us -> 17.3 us
  transfers between devices with their start and end apart: 9 -> 9, of which waited for: 6 -> 7; matrix products, arithmetic and copies ran while one was open for 24% -> 22% of each run, Pallas kernels for 0% -> 0%
where the time goes in v2:
time: 677 us; the launch traced here: 672 us
  other arithmetic  218 us (32%)
  waiting for transfers between devices  143 us (21%)
  Pallas kernels  127 us (19%)
  local copies, waits for them, and re-layouts  85.3 us (13%)
  matrix products  55.9 us (8%)
  starting transfers between devices  41.8 us (6%)
    pallas_call x1, Pallas kernels, slot_sums(): pl.pallas_call(sums_kernel, grid_spec=spec, out_shape=jax.ShapeDtypeStruc...  127 us
    all_to_all x1, waiting for transfers between devices, body(): lax.all_to_all(outgoing, 'slab', split_axis=0, concat_axis=0, tiled=True)  120 us
    another operation x2, other arithmetic, body(): jnp.stack([tall[..., :128], tall[..., half:half + 128], tall[..., 128:]])  75.2 us
    dot_general x4, matrix products, rows_filtered(): jnp.dot(lines, band, precision=lax.Precision.HIGHEST, preferred_element_t...  53 us
    add x2, other arithmetic, tap_sum(): running + weights[tap_index] * lax.slice_in_dim(padded, tap_index, tap_in...  39 us
    another operation x3, other arithmetic, body(): jnp.stack([tap_sum(def_gg, smooth, 0, planes), tap_sum(def_gg, slope, 0,...  34.6 us
    reshape x2, local copies, waits for them, and re-layouts, body(): smoothed.reshape(SUB, sub_y, SUB, sub_x, SUB).transpose(1, 3, 4, 0, 2)  25.2 us
    all_to_all x1, starting transfers between devices, body(): lax.all_to_all(outgoing, 'slab', split_axis=0, concat_axis=0, tiled=True)  22.6 us
  transfers between devices with their start and end apart: 9, of which 7 were waited for; matrix products, arithmetic and copies ran while one was open for 22% of the time, Pallas kernels for 0%

profile of v2, /device:TPU:0, one launch (start us, length us, event | category | flops | bytes accessed | tf_op | source)
XLA Modules:
  0.0 672.5 jit_solution(6119365906567554356)
XLA Ops:
  0.6 5.5 copy.123
  6.1 5.5 copy.124
  11.6 1.3 pad_maximum_fusion.13
  12.9 5.1 collective-permute-start
  18.1 1.3 collective-permute-start.1
  19.4 4.2 collective-permute-done
  23.6 7.6 %collective-permute-done.1 = f32[2,32,256,4]{2,1,3,0:T(8,128)S(1)} collective-permute-done((f32[2,32,256,4]{2,1,3,0:T(8,128)S(1)}, f32[2,32,256,4]{2,1,3,0:T(8,128)S(1)}, u32[]{:S(2)}, u32[]{:S(2)}) %collective-permute-start.1) | collective-permute-done | bytes 262176 | tf_op jit(solution)/shard_map/ppermute | solution.py:25
  31.2 0.4 pad_maximum_fusion.7
  31.5 0.2 copy.125
  31.8 1.4 collective-permute-start.2
  33.1 0.2 copy.126
  33.4 1.5 collective-permute-start.3
  34.8 0.6 collective-permute-done.2
  35.4 0.4 copy.127
  35.9 3.9 collective-permute-done.3
  39.8 0.4 copy.128
  40.2 4.4 pad_maximum_fusion.2
  44.6 4.9 slice_bitcast_fusion.1
  49.6 18.6 %multiply_add_fusion = f32[40,256,128]{1,0,2:T(8,128)} fusion(f32[40,256,136]{1,0,2:T(8,128)} %get-tuple-element.122), kind=kLoop, calls=%fused_computation.66 | loop fusion | flops 22282240 | bytes 52428800 | tf_op jit(solution)/shard_map/add | solution.py:49
  68.2 20.6 %fusion.102 = f32[40,256,128]{1,0,2:T(8,128)} fusion(f32[256,256,1]{1,0,2:T(8,128)S(1)} %copy-done.7, f32[40,256,136]{1,0,2:T(8,128)} %get-tuple-element.122), kind=kOutput, calls=%fused_computation.148 | convolution fusion | flops 4048814080 | bytes 52690944 | tf_op jit(solution)/shard_map/dot_general | solution.py:62
  88.8 6.9 %fusion.96 = f32[40,256,128]{1,0,2:T(8,128)S(1)} fusion(f32[256,256,1]{1,0,2:T(8,128)S(1)} %copy-done.7, f32[40,256,128]{1,0,2:T(8,128)} %multiply_add_fusion), kind=kOutput, calls=%fused_computation.146 | convolution fusion | flops 4026531840 | bytes 10747904 | tf_op jit(solution)/shard_map/dot_general | solution.py:62
  95.7 8.3 %add_bitcast_fusion.1 = (f32[1,32,256,128]{2,1,3,0:T(8,128)}, f32[1,32,256,128]{2,1,3,0:T(8,128)}) fusion(f32[40,256,128]{1,0,2:T(8,128)S(1)} %fusion.96), kind=kLoop, calls=%fused_computation.131 | loop fusion | flops 35651584 | bytes 46137344 | tf_op jit(solution)/shard_map/stack | solution.py:245
  104.0 4.6 fusion.99
  108.6 5.9 fusion.74
  114.5 20.3 %fusion.65 = f32[1,32,256,128]{2,1,3,0:T(8,128)} fusion(f32[40,256,128]{1,0,2:T(8,128)} %fusion.102), kind=kLoop, calls=%fused_computation.95 | loop fusion | flops 17825792 | bytes 41943040 | tf_op jit(solution)/shard_map/stack | solution.py:245
  134.9 1.2 pad_maximum_fusion.11
  136.1 3.7 collective-permute-start.4
  139.8 1.4 collective-permute-start.5
  141.2 2.4 collective-permute-done.4
  143.6 4.6 collective-permute-done.5
  148.2 7.0 %maximum_bitcast_fusion = f32[4,132,32,256]{3,2,1,0:T(8,128)} fusion(f32[4,32,256,2]{2,1,3,0:T(8,128)S(1)} %collective-permute-done.5, f32[1,32,256,128]{2,1,3,0:T(8,128)S(1)} %copy-done.4, f32[1,32,256,128]{2,1,3,0:T(8,128)S(1)} %copy-done.3, f32[1,32,256,128]{2,1,3,0:T(8,128)S(1)} %copy-done.6, f32[1,32,256,128]{2,1,3,0:T(8,128)S(1)} %copy-done.5, ...), kind=kLoop, calls=%fused_computation.15 | loop fusion | flops 21626880 | bytes 34603008 | tf_op jit(solution)/shard_map/transpose | solution.py:287
  155.2 1.3 collective-permute-start.6
  156.8 0.3 convert_reduce_fusion.2
  157.1 20.9 %fusion.105 = f32[40,256,128]{1,0,2:T(8,128)} fusion(f32[256,256,1]{1,0,2:T(8,128)S(1)} %copy-done.7, f32[40,256,136]{1,0,2:T(8,128)} %get-tuple-element.123), kind=kOutput, calls=%fused_computation.149 | convolution fusion | flops 4048814080 | bytes 52690944 | tf_op jit(solution)/shard_map/dot_general | solution.py:62
  178.0 20.4 %fusion.56 = f32[32,256,128]{1,0,2:T(8,128)} fusion(f32[40,256,128]{1,0,2:T(8,128)} %fusion.105), kind=kLoop, calls=%fused_computation.77 | loop fusion | flops 17825792 | bytes 41943040 | tf_op jit(solution)/shard_map/add | solution.py:49
  198.5 10.9 %reshape.5665 = f32[32,8,32,4,32]{2,1,0,4,3:T(8,128)} reshape(f32[32,256,128]{1,0,2:T(8,128)} %fusion.56) | data formatting | bytes 8388608 | tf_op jit(solution)/shard_map/reshape | solution.py:259
  209.4 14.3 %copy.160 = f32[32,8,32,4,32]{2,0,4,3,1:T(8,128)} copy(f32[32,8,32,4,32]{2,1,0,4,3:T(8,128)} %reshape.5665) | data formatting | bytes 8388608 | tf_op jit(solution)/shard_map/reshape | solution.py:259
  223.7 9.4 %fusion.306 = f32[8,4]{1,0:T(8,128)S(1)} fusion(f32[32,8,32,4,32]{2,1,0,4,3:T(8,128)} %reshape.5665), kind=kLoop, calls=%fused_computation.645 | loop fusion | flops 1048544 | bytes 4194432 | tf_op jit(solution)/shard_map/reduce_sum | solution.py:263
  233.2 10.1 %multiply_reduce_fusion = f32[8,4]{1,0:T(8,128)S(1)} fusion(f32[8,4]{1,0:T(8,128)S(1)} %broadcast_multiply_fusion, f32[32,8,32,4,32]{2,1,0,4,3:T(8,128)} %reshape.5665), kind=kLoop, calls=%fused_computation.19 | loop fusion | flops 3145696 | bytes 4194560 | tf_op jit(solution)/shard_map/reduce_sum | solution.py:266
  243.4 11.6 %reshape.5666 = f32[32,32768]{1,0:T(8,128)} reshape(f32[8,4,32,32,32]{4,3,2,1,0:T(8,128)} %bitcast.303) | data formatting | bytes 8388608 | tf_op jit(solution)/shard_map/reshape | solution.py:261
  255.0 2.9 convolution_convert_fusion
  257.9 2.2 reshape.5667
  260.1 22.6 %all-to-all-start = ((bf16[8,4,32768]{2,1,0:T(4,128)(2,1)}), bf16[8,4,32768]{2,1,0:T(4,128)(2,1)S(1)}, u32[]{:S(2)}, u32[]{:S(2)}) async-start(bf16[8,4,32768]{2,1,0:T(4,128)(2,1)} %reshape.5667), calls=%async_computation | async-start | bytes 4194304 | tf_op jit(solution)/shard_map/all_to_all | solution.py:285
  282.7 0.7 multiply_reduce_fusion.1
  284.0 0.3 select_reduce_fusion
  285.6 0.2 convert_reduce_fusion.1
  287.4 119.5 %all-to-all-done = bf16[8,4,32768]{2,1,0:T(4,128)(2,1)S(1)} async-done(((bf16[8,4,32768]{2,1,0:T(4,128)(2,1)}), bf16[8,4,32768]{2,1,0:T(4,128)(2,1)S(1)}, u32[]{:S(2)}, u32[]{:S(2)}) %all-to-all-start) | async-done | bytes 2097184 | tf_op jit(solution)/shard_map/all_to_all | solution.py:285
  406.9 6.9 %reshape.5668 = bf16[32,32,32,32]{3,2,1,0:T(8,128)(2,1)} reshape(bf16[8,4,32768]{2,1,0:T(4,128)(2,1)S(1)} %all-to-all-done) | data formatting | bytes 4194304 | tf_op jit(solution)/shard_map/reshape | solution.py:292
  413.8 21.2 %pad_maximum_fusion.3.ref_ref = bf16[32,32,32,128]{3,2,1,0:T(8,128)(2,1)} fusion(bf16[32,32,32,32]{3,2,1,0:T(8,128)(2,1)} %reshape.5668), kind=kLoop, calls=%fused_computation.21 | loop fusion | flops 33554432 | bytes 10485760 | tf_op jit(solution)/shard_map/concatenate | solution.py:293
  435.0 39.8 %fusion.3 = (f32[1,4,132,64,128]{4,3,2,1,0:T(8,128)}, f32[1,4,132,64,128]{4,3,2,1,0:T(8,128)}, f32[1,4,132,64,128]{4,3,2,1,0:T(8,128)}) fusion(f32[4,132,32,256]{3,2,1,0:T(8,128)} %maximum_bitcast_fusion, f32[4,132,32,256]{3,2,1,0:T(8,128)} %collective-permute-done.6), kind=kLoop, calls=%fused_computation.12 | loop fusion | flops 12976128 | bytes 86507520 | tf_op jit(solution)/shard_map/stack | solution.py:291
  474.9 35.3 %pad_maximum_fusion.field_ref = f32[3,4,132,64,128]{4,3,2,1,0:T(8,128)} fusion(f32[1,4,132,64,128]{4,3,2,1,0:T(8,128)} %get-tuple-element.118, f32[1,4,132,64,128]{4,3,2,1,0:T(8,128)} %get-tuple-element.119, f32[1,4,132,64,128]{4,3,2,1,0:T(8,128)} %get-tuple-element.117), kind=kLoop, calls=%fused_computation.1 | loop fusion | flops 25952256 | bytes 103809024 | tf_op jit(solution)/shard_map/stack | solution.py:291
  510.2 3.4 copy-done
  513.6 127.2 %shard_map.94 = f32[96,18,128]{2,1,0:T(8,128)S(1)} custom-call(s32[96]{0:T(128)S(1)} %reshape.5662.x_first, s32[96]{0:T(128)S(1)} %get-tuple-element.114.z_tile, s32[96]{0:T(128)S(1)} %get-tuple-element.113.z_in, s32[96]{0:T(128)S(1)} %get-tuple-element.277.y_part, s32[96]{0:T(128)S(1)} %get-tuple-element.276.y_in, ...), custom_call_target="tpu_custom_call" | custom-call | tf_op jit(solution)/shard_map/pallas_call | solution.py:208
  640.8 0.4 reduce_sum.97
  641.2 0.7 reshape.6287
  641.9 3.6 all-to-all-start.1
  645.5 10.6 %fusion.5 = (f32[8,4]{1,0:T(8,128)S(1)}, f32[8,4]{1,0:T(8,128)S(1)}) fusion(f32[8,4]{1,0:T(8,128)S(1)} %add_sqrt_fusion, f32[8,4]{1,0:T(8,128)S(1)} %broadcast_multiply_fusion, f32[32,8,32,4,32]{2,1,0,4,3:T(8,128)} %reshape.5665), kind=kLoop, calls=%fused_computation.16 | loop fusion | flops 7339968 | bytes 4194816 | tf_op jit(solution)/shard_map/reduce_sum | solution.py:295
  656.2 0.5 broadcast.1430
  656.8 0.7 reduce.460
  657.5 0.7 gather_fusion
  658.8 0.7 copy.143
  665.3 0.7 copy.142
  671.3 0.1 divide_subtract_fusion.2
  671.5 0.7 copy.141
  (266 shorter events, 15.6 us)
Async XLA Ops:
  11.6 19.5 %copy-start.1 = (f32[32,256,128]{1,0,2:T(8,128)S(1)}, f32[32,256,128]{1,0,2:T(8,128)}, u32[]{:S(2)}) copy-start(f32[32,256,128]{1,0,2:T(8,128)} %copy.123) | copy-start | bytes 12582916
  11.6 19.5 %copy-start.2 = (f32[32,256,128]{1,0,2:T(8,128)S(1)}, f32[32,256,128]{1,0,2:T(8,128)}, u32[]{:S(2)}) copy-start(f32[32,256,128]{1,0,2:T(8,128)} %copy.124) | copy-start | bytes 12582916
  12.9 10.7 %collective-permute-start = (f32[2,32,256,4]{2,1,3,0:T(8,128)S(1)}, f32[2,32,256,4]{2,1,3,0:T(8,128)S(1)}, u32[]{:S(2)}, u32[]{:S(2)}) collective-permute-start(f32[2,32,256,4]{2,1,3,0:T(8,128)S(1)} %get-tuple-element.126), channel_id=1, source_target_pairs={{0,8},{8,16},{16,24},{1,9},{9,17},{17,25},{2,10},{10,18},{18,26},{... | collective-permute-start | bytes 786440 | tf_op jit(solution)/shard_map/ppermute | solution.py:24
  18.1 13.1 %collective-permute-start.1 = (f32[2,32,256,4]{2,1,3,0:T(8,128)S(1)}, f32[2,32,256,4]{2,1,3,0:T(8,128)S(1)}, u32[]{:S(2)}, u32[]{:S(2)}) collective-permute-start(f32[2,32,256,4]{2,1,3,0:T(8,128)S(1)} %get-tuple-element.127), channel_id=1, source_target_pairs={{8,0},{16,8},{24,16},{9,1},{17,9},{25,17},{10,2},{18,10},{26,18},{... | collective-permute-start | bytes 786440 | tf_op jit(solution)/shard_map/ppermute | solution.py:25
  31.8 3.7 collective-permute-start.2
  33.4 6.4 collective-permute-start.3
  49.6 18.6 %copy-start.7 = (f32[256,256,1]{1,0,2:T(8,128)S(1)}, f32[256,256,1]{1,0,2:T(8,128)}, u32[]{:S(2)}) copy-start(f32[256,256,1]{1,0,2:T(8,128)} %constant.189) | copy-start | bytes 786436
  88.8 15.3 %slice-start = ((s8[5242880]{0:T(1024)(128)(4,1)}), s8[4194304]{0:T(1024)(128)(4,1)S(1)}, s32[]{:S(2)}) async-start(s8[5242880]{0:T(1024)(128)(4,1)} %bitcast.310), calls=%async_computation.2 | async-start | bytes 8388608
  95.7 8.4 %slice-start.1 = ((s8[5242880]{0:T(1024)(128)(4,1)}), s8[1048576]{0:T(1024)(128)(4,1)S(1)}, s32[]{:S(2)}) async-start(s8[5242880]{0:T(1024)(128)(4,1)} %bitcast.310), calls=%async_computation.3 | async-start | bytes 2097152
  95.7 8.3 %copy-start.8 = (f32[256,256,1]{1,0,2:T(8,128)S(1)}, f32[256,256,1]{1,0,2:T(8,128)}, u32[]{:S(2)}) copy-start(f32[256,256,1]{1,0,2:T(8,128)} %constant.190) | copy-start | bytes 786436
  114.5 20.3 %copy-start.3 = (f32[1,32,256,128]{2,1,3,0:T(8,128)S(1)}, f32[1,32,256,128]{2,1,3,0:T(8,128)}, u32[]{:S(2)}) copy-start(f32[1,32,256,128]{2,1,3,0:T(8,128)} %fusion.74) | copy-start | bytes 12582916
  134.9 13.3 %copy-start.4 = (f32[1,32,256,128]{2,1,3,0:T(8,128)S(1)}, f32[1,32,256,128]{2,1,3,0:T(8,128)}, u32[]{:S(2)}) copy-start(f32[1,32,256,128]{2,1,3,0:T(8,128)} %fusion.65) | copy-start | bytes 12582916
  134.9 13.3 %copy-start.5 = (f32[1,32,256,128]{2,1,3,0:T(8,128)S(1)}, f32[1,32,256,128]{2,1,3,0:T(8,128)}, u32[]{:S(2)}) copy-start(f32[1,32,256,128]{2,1,3,0:T(8,128)} %get-tuple-element.128) | copy-start | bytes 12582916
  134.9 13.3 %copy-start.6 = (f32[1,32,256,128]{2,1,3,0:T(8,128)S(1)}, f32[1,32,256,128]{2,1,3,0:T(8,128)}, u32[]{:S(2)}) copy-start(f32[1,32,256,128]{2,1,3,0:T(8,128)} %get-tuple-element.129) | copy-start | bytes 12582916
  136.1 7.5 %collective-permute-start.4 = (f32[4,32,256,2]{2,1,3,0:T(8,128)S(1)}, f32[4,32,256,2]{2,1,3,0:T(8,128)S(1)}, u32[]{:S(2)}, u32[]{:S(2)}) collective-permute-start(f32[4,32,256,2]{2,1,3,0:T(8,128)S(1)} %get-tuple-element.120), channel_id=1, source_target_pairs={{0,8},{8,16},{16,24},{1,9},{9,17},{17,25},{2,10},{10,18},{18,26},{... | collective-permute-start | bytes 786440 | tf_op jit(solution)/shard_map/ppermute | solution.py:24
  139.8 16.7 %copy-start.9 = (s32[3,3,8,8,4]{3,4,2,1,0:T(4,128)S(1)}, s32[3,3,8,8,4]{3,4,2,1,0:T(4,128)}, u32[]{:S(2)}) copy-start(s32[3,3,8,8,4]{3,4,2,1,0:T(4,128)} %param.9) | copy-start | bytes 27652
  139.8 8.4 %collective-permute-start.5 = (f32[4,32,256,2]{2,1,3,0:T(8,128)S(1)}, f32[4,32,256,2]{2,1,3,0:T(8,128)S(1)}, u32[]{:S(2)}, u32[]{:S(2)}) collective-permute-start(f32[4,32,256,2]{2,1,3,0:T(8,128)S(1)} %get-tuple-element.121), channel_id=1, source_target_pairs={{8,0},{16,8},{24,16},{9,1},{17,9},{25,17},{10,2},{18,10},{26,18},{... | collective-permute-start | bytes 786440 | tf_op jit(solution)/shard_map/ppermute | solution.py:25
  155.2 279.8 %collective-permute-start.6 = (f32[4,132,32,256]{3,2,1,0:T(8,128)}, f32[4,132,32,256]{3,2,1,0:T(8,128)}, u32[]{:S(2)}, u32[]{:S(2)}) collective-permute-start(f32[4,132,32,256]{3,2,1,0:T(8,128)} %maximum_bitcast_fusion), channel_id=1, source_target_pairs={{1,0},{2,1},{3,2},{4,3},{5,4},{6,5},{7,6},{9,8},{10,9},{11,10},{12... | collective-permute-start | bytes 51904520 | tf_op jit(solution)/shard_map/ppermute | solution.py:33
  260.1 146.7 %all-to-all-start = ((bf16[8,4,32768]{2,1,0:T(4,128)(2,1)}), bf16[8,4,32768]{2,1,0:T(4,128)(2,1)S(1)}, u32[]{:S(2)}, u32[]{:S(2)}) async-start(bf16[8,4,32768]{2,1,0:T(4,128)(2,1)} %reshape.5667), calls=%async_computation | async-start | bytes 4194304 | tf_op jit(solution)/shard_map/all_to_all | solution.py:285
  510.2 3.4 copy-start
  641.9 14.3 %all-to-all-start.1 = ((f32[8,1,216]{2,1,0:T(1,128)}), f32[8,1,216]{2,1,0:T(1,128)S(1)}, u32[]{:S(2)}, u32[]{:S(2)}) async-start(f32[8,1,216]{2,1,0:T(1,128)} %reshape.6287), calls=%async_computation.1 | async-start | bytes 16384 | tf_op jit(solution)/shard_map/all_to_all | solution.py:297

commit v3 on v2

--- a/solution.py
+++ b/solution.py
@@ -177,7 +177,7 @@
         return tuple(acc)
 
     zero = jnp.zeros((8, 128), jnp.float32)
-    acc = lax.fori_loop(0, SUB, plane, (zero,) * SUMS, unroll=4)
+    acc = lax.fori_loop(0, SUB, plane, (zero,) * SUMS, unroll=8)
     lane = lax.broadcasted_iota(jnp.int32, (1, 128), 1)
     inside = (lane >= y_off) & (lane < y_off + SUB)
     for n in range(SUMS):

time: 677 us -> 671 us (level)
  no operation moved by 1% of the time
where the time goes in v3:
time: 671 us; the launch traced here: 667 us
  other arithmetic  218 us (32%)
  waiting for transfers between devices  143 us (21%)
  Pallas kernels  122 us (18%)
  local copies, waits for them, and re-layouts  85.3 us (13%)
  matrix products  55.9 us (8%)
  starting transfers between devices  41.8 us (6%)
    pallas_call x1, Pallas kernels, slot_sums(): pl.pallas_call(sums_kernel, grid_spec=spec, out_shape=jax.ShapeDtypeStruc...  122 us
    all_to_all x1, waiting for transfers between devices, body(): lax.all_to_all(outgoing, 'slab', split_axis=0, concat_axis=0, tiled=True)  120 us
    another operation x2, other arithmetic, body(): jnp.stack([tall[..., :128], tall[..., half:half + 128], tall[..., 128:]])  75.2 us
    dot_general x4, matrix products, rows_filtered(): jnp.dot(lines, band, precision=lax.Precision.HIGHEST, preferred_element_t...  53 us
    add x2, other arithmetic, tap_sum(): running + weights[tap_index] * lax.slice_in_dim(padded, tap_index, tap_in...  39 us
    another operation x3, other arithmetic, body(): jnp.stack([tap_sum(def_gg, smooth, 0, planes), tap_sum(def_gg, slope, 0,...  34.6 us
    reshape x2, local copies, waits for them, and re-layouts, body(): smoothed.reshape(SUB, sub_y, SUB, sub_x, SUB).transpose(1, 3, 4, 0, 2)  25.2 us
    all_to_all x1, starting transfers between devices, body(): lax.all_to_all(outgoing, 'slab', split_axis=0, concat_axis=0, tiled=True)  22.6 us
  transfers between devices with their start and end apart: 9, of which 7 were waited for; matrix products, arithmetic and copies ran while one was open for 22% of the time, Pallas kernels for 0%

profile of v3, /device:TPU:0, one launch (start us, length us, event | category | flops | bytes accessed | tf_op | source)
XLA Modules:
  0.0 667.4 jit_solution(6719602799284861284)
XLA Ops:
  0.6 5.5 copy.123
  6.1 5.5 copy.124
  11.6 1.3 pad_maximum_fusion.13
  12.9 5.1 collective-permute-start
  18.1 1.3 collective-permute-start.1
  19.4 4.2 collective-permute-done
  23.6 7.6 %collective-permute-done.1 = f32[2,32,256,4]{2,1,3,0:T(8,128)S(1)} collective-permute-done((f32[2,32,256,4]{2,1,3,0:T(8,128)S(1)}, f32[2,32,256,4]{2,1,3,0:T(8,128)S(1)}, u32[]{:S(2)}, u32[]{:S(2)}) %collective-permute-start.1) | collective-permute-done | bytes 262176 | tf_op jit(solution)/shard_map/ppermute | solution.py:25
  31.2 0.4 pad_maximum_fusion.7
  31.5 0.2 copy.125
  31.8 1.4 collective-permute-start.2
  33.1 0.2 copy.126
  33.4 1.5 collective-permute-start.3
  34.8 0.6 collective-permute-done.2
  35.4 0.4 copy.127
  35.9 3.9 collective-permute-done.3
  39.8 0.4 copy.128
  40.2 4.4 pad_maximum_fusion.2
  44.6 4.9 slice_bitcast_fusion.1
  49.6 18.6 %multiply_add_fusion = f32[40,256,128]{1,0,2:T(8,128)} fusion(f32[40,256,136]{1,0,2:T(8,128)} %get-tuple-element.122), kind=kLoop, calls=%fused_computation.66 | loop fusion | flops 22282240 | bytes 52428800 | tf_op jit(solution)/shard_map/add | solution.py:49
  68.2 20.6 %fusion.102 = f32[40,256,128]{1,0,2:T(8,128)} fusion(f32[256,256,1]{1,0,2:T(8,128)S(1)} %copy-done.7, f32[40,256,136]{1,0,2:T(8,128)} %get-tuple-element.122), kind=kOutput, calls=%fused_computation.148 | convolution fusion | flops 4048814080 | bytes 52690944 | tf_op jit(solution)/shard_map/dot_general | solution.py:62
  88.8 6.9 %fusion.96 = f32[40,256,128]{1,0,2:T(8,128)S(1)} fusion(f32[256,256,1]{1,0,2:T(8,128)S(1)} %copy-done.7, f32[40,256,128]{1,0,2:T(8,128)} %multiply_add_fusion), kind=kOutput, calls=%fused_computation.146 | convolution fusion | flops 4026531840 | bytes 10747904 | tf_op jit(solution)/shard_map/dot_general | solution.py:62
  95.7 8.3 %add_bitcast_fusion.1 = (f32[1,32,256,128]{2,1,3,0:T(8,128)}, f32[1,32,256,128]{2,1,3,0:T(8,128)}) fusion(f32[40,256,128]{1,0,2:T(8,128)S(1)} %fusion.96), kind=kLoop, calls=%fused_computation.131 | loop fusion | flops 35651584 | bytes 46137344 | tf_op jit(solution)/shard_map/stack | solution.py:245
  104.0 4.6 fusion.99
  108.6 5.9 fusion.74
  114.5 20.3 %fusion.65 = f32[1,32,256,128]{2,1,3,0:T(8,128)} fusion(f32[40,256,128]{1,0,2:T(8,128)} %fusion.102), kind=kLoop, calls=%fused_computation.95 | loop fusion | flops 17825792 | bytes 41943040 | tf_op jit(solution)/shard_map/stack | solution.py:245
  134.9 1.2 pad_maximum_fusion.11
  136.1 3.7 collective-permute-start.4
  139.8 1.4 collective-permute-start.5
  141.2 2.4 collective-permute-done.4
  143.6 4.6 collective-permute-done.5
  148.2 7.0 %maximum_bitcast_fusion = f32[4,132,32,256]{3,2,1,0:T(8,128)} fusion(f32[4,32,256,2]{2,1,3,0:T(8,128)S(1)} %collective-permute-done.5, f32[1,32,256,128]{2,1,3,0:T(8,128)S(1)} %copy-done.4, f32[1,32,256,128]{2,1,3,0:T(8,128)S(1)} %copy-done.3, f32[1,32,256,128]{2,1,3,0:T(8,128)S(1)} %copy-done.6, f32[1,32,256,128]{2,1,3,0:T(8,128)S(1)} %copy-done.5, ...), kind=kLoop, calls=%fused_computation.15 | loop fusion | flops 21626880 | bytes 34603008 | tf_op jit(solution)/shard_map/transpose | solution.py:287
  155.2 1.3 collective-permute-start.6
  156.8 0.3 convert_reduce_fusion.2
  157.1 20.9 %fusion.105 = f32[40,256,128]{1,0,2:T(8,128)} fusion(f32[256,256,1]{1,0,2:T(8,128)S(1)} %copy-done.7, f32[40,256,136]{1,0,2:T(8,128)} %get-tuple-element.123), kind=kOutput, calls=%fused_computation.149 | convolution fusion | flops 4048814080 | bytes 52690944 | tf_op jit(solution)/shard_map/dot_general | solution.py:62
  178.0 20.4 %fusion.56 = f32[32,256,128]{1,0,2:T(8,128)} fusion(f32[40,256,128]{1,0,2:T(8,128)} %fusion.105), kind=kLoop, calls=%fused_computation.77 | loop fusion | flops 17825792 | bytes 41943040 | tf_op jit(solution)/shard_map/add | solution.py:49
  198.5 10.9 %reshape.5665 = f32[32,8,32,4,32]{2,1,0,4,3:T(8,128)} reshape(f32[32,256,128]{1,0,2:T(8,128)} %fusion.56) | data formatting | bytes 8388608 | tf_op jit(solution)/shard_map/reshape | solution.py:259
  209.4 14.3 %copy.160 = f32[32,8,32,4,32]{2,0,4,3,1:T(8,128)} copy(f32[32,8,32,4,32]{2,1,0,4,3:T(8,128)} %reshape.5665) | data formatting | bytes 8388608 | tf_op jit(solution)/shard_map/reshape | solution.py:259
  223.7 9.4 %fusion.306 = f32[8,4]{1,0:T(8,128)S(1)} fusion(f32[32,8,32,4,32]{2,1,0,4,3:T(8,128)} %reshape.5665), kind=kLoop, calls=%fused_computation.645 | loop fusion | flops 1048544 | bytes 4194432 | tf_op jit(solution)/shard_map/reduce_sum | solution.py:263
  233.2 10.1 %multiply_reduce_fusion = f32[8,4]{1,0:T(8,128)S(1)} fusion(f32[8,4]{1,0:T(8,128)S(1)} %broadcast_multiply_fusion, f32[32,8,32,4,32]{2,1,0,4,3:T(8,128)} %reshape.5665), kind=kLoop, calls=%fused_computation.19 | loop fusion | flops 3145696 | bytes 4194560 | tf_op jit(solution)/shard_map/reduce_sum | solution.py:266
  243.4 11.6 %reshape.5666 = f32[32,32768]{1,0:T(8,128)} reshape(f32[8,4,32,32,32]{4,3,2,1,0:T(8,128)} %bitcast.303) | data formatting | bytes 8388608 | tf_op jit(solution)/shard_map/reshape | solution.py:261
  255.0 2.9 convolution_convert_fusion
  257.9 2.2 reshape.5667
  260.1 22.6 %all-to-all-start = ((bf16[8,4,32768]{2,1,0:T(4,128)(2,1)}), bf16[8,4,32768]{2,1,0:T(4,128)(2,1)S(1)}, u32[]{:S(2)}, u32[]{:S(2)}) async-start(bf16[8,4,32768]{2,1,0:T(4,128)(2,1)} %reshape.5667), calls=%async_computation | async-start | bytes 4194304 | tf_op jit(solution)/shard_map/all_to_all | solution.py:285
  282.7 0.7 multiply_reduce_fusion.1
  284.0 0.3 select_reduce_fusion
  285.6 0.2 convert_reduce_fusion.1
  287.4 119.5 %all-to-all-done = bf16[8,4,32768]{2,1,0:T(4,128)(2,1)S(1)} async-done(((bf16[8,4,32768]{2,1,0:T(4,128)(2,1)}), bf16[8,4,32768]{2,1,0:T(4,128)(2,1)S(1)}, u32[]{:S(2)}, u32[]{:S(2)}) %all-to-all-start) | async-done | bytes 2097184 | tf_op jit(solution)/shard_map/all_to_all | solution.py:285
  406.9 6.9 %reshape.5668 = bf16[32,32,32,32]{3,2,1,0:T(8,128)(2,1)} reshape(bf16[8,4,32768]{2,1,0:T(4,128)(2,1)S(1)} %all-to-all-done) | data formatting | bytes 4194304 | tf_op jit(solution)/shard_map/reshape | solution.py:292
  413.8 21.2 %pad_maximum_fusion.3.ref_ref = bf16[32,32,32,128]{3,2,1,0:T(8,128)(2,1)} fusion(bf16[32,32,32,32]{3,2,1,0:T(8,128)(2,1)} %reshape.5668), kind=kLoop, calls=%fused_computation.21 | loop fusion | flops 33554432 | bytes 10485760 | tf_op jit(solution)/shard_map/concatenate | solution.py:293
  435.0 39.8 %fusion.3 = (f32[1,4,132,64,128]{4,3,2,1,0:T(8,128)}, f32[1,4,132,64,128]{4,3,2,1,0:T(8,128)}, f32[1,4,132,64,128]{4,3,2,1,0:T(8,128)}) fusion(f32[4,132,32,256]{3,2,1,0:T(8,128)} %maximum_bitcast_fusion, f32[4,132,32,256]{3,2,1,0:T(8,128)} %collective-permute-done.6), kind=kLoop, calls=%fused_computation.12 | loop fusion | flops 12976128 | bytes 86507520 | tf_op jit(solution)/shard_map/stack | solution.py:291
  474.9 35.3 %pad_maximum_fusion.field_ref = f32[3,4,132,64,128]{4,3,2,1,0:T(8,128)} fusion(f32[1,4,132,64,128]{4,3,2,1,0:T(8,128)} %get-tuple-element.118, f32[1,4,132,64,128]{4,3,2,1,0:T(8,128)} %get-tuple-element.119, f32[1,4,132,64,128]{4,3,2,1,0:T(8,128)} %get-tuple-element.117), kind=kLoop, calls=%fused_computation.1 | loop fusion | flops 25952256 | bytes 103809024 | tf_op jit(solution)/shard_map/stack | solution.py:291
  510.2 3.4 copy-done
  513.6 122.1 %shard_map.94 = f32[96,18,128]{2,1,0:T(8,128)S(1)} custom-call(s32[96]{0:T(128)S(1)} %reshape.5662.x_first, s32[96]{0:T(128)S(1)} %get-tuple-element.114.z_tile, s32[96]{0:T(128)S(1)} %get-tuple-element.113.z_in, s32[96]{0:T(128)S(1)} %get-tuple-element.277.y_part, s32[96]{0:T(128)S(1)} %get-tuple-element.276.y_in, ...), custom_call_target="tpu_custom_call" | custom-call | tf_op jit(solution)/shard_map/pallas_call | solution.py:208
  635.7 0.4 reduce_sum.97
  636.1 0.7 reshape.6287
  636.8 3.6 all-to-all-start.1
  640.4 10.6 %fusion.5 = (f32[8,4]{1,0:T(8,128)S(1)}, f32[8,4]{1,0:T(8,128)S(1)}) fusion(f32[8,4]{1,0:T(8,128)S(1)} %add_sqrt_fusion, f32[8,4]{1,0:T(8,128)S(1)} %broadcast_multiply_fusion, f32[32,8,32,4,32]{2,1,0,4,3:T(8,128)} %reshape.5665), kind=kLoop, calls=%fused_computation.16 | loop fusion | flops 7339968 | bytes 4194816 | tf_op jit(solution)/shard_map/reduce_sum | solution.py:295
  651.1 0.5 broadcast.1430
  651.7 0.7 reduce.460
  652.4 0.7 gather_fusion
  653.7 0.7 copy.143
  660.2 0.7 copy.142
  666.3 0.1 divide_subtract_fusion.2
  666.4 0.7 copy.141
  (266 shorter events, 15.6 us)
Async XLA Ops:
  11.6 19.5 %copy-start.1 = (f32[32,256,128]{1,0,2:T(8,128)S(1)}, f32[32,256,128]{1,0,2:T(8,128)}, u32[]{:S(2)}) copy-start(f32[32,256,128]{1,0,2:T(8,128)} %copy.123) | copy-start | bytes 12582916
  11.6 19.5 %copy-start.2 = (f32[32,256,128]{1,0,2:T(8,128)S(1)}, f32[32,256,128]{1,0,2:T(8,128)}, u32[]{:S(2)}) copy-start(f32[32,256,128]{1,0,2:T(8,128)} %copy.124) | copy-start | bytes 12582916
  12.9 10.7 %collective-permute-start = (f32[2,32,256,4]{2,1,3,0:T(8,128)S(1)}, f32[2,32,256,4]{2,1,3,0:T(8,128)S(1)}, u32[]{:S(2)}, u32[]{:S(2)}) collective-permute-start(f32[2,32,256,4]{2,1,3,0:T(8,128)S(1)} %get-tuple-element.126), channel_id=1, source_target_pairs={{0,8},{8,16},{16,24},{1,9},{9,17},{17,25},{2,10},{10,18},{18,26},{... | collective-permute-start | bytes 786440 | tf_op jit(solution)/shard_map/ppermute | solution.py:24
  18.1 13.1 %collective-permute-start.1 = (f32[2,32,256,4]{2,1,3,0:T(8,128)S(1)}, f32[2,32,256,4]{2,1,3,0:T(8,128)S(1)}, u32[]{:S(2)}, u32[]{:S(2)}) collective-permute-start(f32[2,32,256,4]{2,1,3,0:T(8,128)S(1)} %get-tuple-element.127), channel_id=1, source_target_pairs={{8,0},{16,8},{24,16},{9,1},{17,9},{25,17},{10,2},{18,10},{26,18},{... | collective-permute-start | bytes 786440 | tf_op jit(solution)/shard_map/ppermute | solution.py:25
  31.8 3.7 collective-permute-start.2
  33.4 6.4 collective-permute-start.3
  49.6 18.6 %copy-start.7 = (f32[256,256,1]{1,0,2:T(8,128)S(1)}, f32[256,256,1]{1,0,2:T(8,128)}, u32[]{:S(2)}) copy-start(f32[256,256,1]{1,0,2:T(8,128)} %constant.189) | copy-start | bytes 786436
  88.8 15.3 %slice-start = ((s8[5242880]{0:T(1024)(128)(4,1)}), s8[4194304]{0:T(1024)(128)(4,1)S(1)}, s32[]{:S(2)}) async-start(s8[5242880]{0:T(1024)(128)(4,1)} %bitcast.310), calls=%async_computation.2 | async-start | bytes 8388608
  95.7 8.4 %slice-start.1 = ((s8[5242880]{0:T(1024)(128)(4,1)}), s8[1048576]{0:T(1024)(128)(4,1)S(1)}, s32[]{:S(2)}) async-start(s8[5242880]{0:T(1024)(128)(4,1)} %bitcast.310), calls=%async_computation.3 | async-start | bytes 2097152
  95.7 8.3 %copy-start.8 = (f32[256,256,1]{1,0,2:T(8,128)S(1)}, f32[256,256,1]{1,0,2:T(8,128)}, u32[]{:S(2)}) copy-start(f32[256,256,1]{1,0,2:T(8,128)} %constant.190) | copy-start | bytes 786436
  114.5 20.3 %copy-start.3 = (f32[1,32,256,128]{2,1,3,0:T(8,128)S(1)}, f32[1,32,256,128]{2,1,3,0:T(8,128)}, u32[]{:S(2)}) copy-start(f32[1,32,256,128]{2,1,3,0:T(8,128)} %fusion.74) | copy-start | bytes 12582916
  134.9 13.3 %copy-start.4 = (f32[1,32,256,128]{2,1,3,0:T(8,128)S(1)}, f32[1,32,256,128]{2,1,3,0:T(8,128)}, u32[]{:S(2)}) copy-start(f32[1,32,256,128]{2,1,3,0:T(8,128)} %fusion.65) | copy-start | bytes 12582916
  134.9 13.3 %copy-start.5 = (f32[1,32,256,128]{2,1,3,0:T(8,128)S(1)}, f32[1,32,256,128]{2,1,3,0:T(8,128)}, u32[]{:S(2)}) copy-start(f32[1,32,256,128]{2,1,3,0:T(8,128)} %get-tuple-element.128) | copy-start | bytes 12582916
  134.9 13.3 %copy-start.6 = (f32[1,32,256,128]{2,1,3,0:T(8,128)S(1)}, f32[1,32,256,128]{2,1,3,0:T(8,128)}, u32[]{:S(2)}) copy-start(f32[1,32,256,128]{2,1,3,0:T(8,128)} %get-tuple-element.129) | copy-start | bytes 12582916
  136.1 7.5 %collective-permute-start.4 = (f32[4,32,256,2]{2,1,3,0:T(8,128)S(1)}, f32[4,32,256,2]{2,1,3,0:T(8,128)S(1)}, u32[]{:S(2)}, u32[]{:S(2)}) collective-permute-start(f32[4,32,256,2]{2,1,3,0:T(8,128)S(1)} %get-tuple-element.120), channel_id=1, source_target_pairs={{0,8},{8,16},{16,24},{1,9},{9,17},{17,25},{2,10},{10,18},{18,26},{... | collective-permute-start | bytes 786440 | tf_op jit(solution)/shard_map/ppermute | solution.py:24
  139.8 16.7 %copy-start.9 = (s32[3,3,8,8,4]{3,4,2,1,0:T(4,128)S(1)}, s32[3,3,8,8,4]{3,4,2,1,0:T(4,128)}, u32[]{:S(2)}) copy-start(s32[3,3,8,8,4]{3,4,2,1,0:T(4,128)} %param.9) | copy-start | bytes 27652
  139.8 8.4 %collective-permute-start.5 = (f32[4,32,256,2]{2,1,3,0:T(8,128)S(1)}, f32[4,32,256,2]{2,1,3,0:T(8,128)S(1)}, u32[]{:S(2)}, u32[]{:S(2)}) collective-permute-start(f32[4,32,256,2]{2,1,3,0:T(8,128)S(1)} %get-tuple-element.121), channel_id=1, source_target_pairs={{8,0},{16,8},{24,16},{9,1},{17,9},{25,17},{10,2},{18,10},{26,18},{... | collective-permute-start | bytes 786440 | tf_op jit(solution)/shard_map/ppermute | solution.py:25
  155.2 279.8 %collective-permute-start.6 = (f32[4,132,32,256]{3,2,1,0:T(8,128)}, f32[4,132,32,256]{3,2,1,0:T(8,128)}, u32[]{:S(2)}, u32[]{:S(2)}) collective-permute-start(f32[4,132,32,256]{3,2,1,0:T(8,128)} %maximum_bitcast_fusion), channel_id=1, source_target_pairs={{1,0},{2,1},{3,2},{4,3},{5,4},{6,5},{7,6},{9,8},{10,9},{11,10},{12... | collective-permute-start | bytes 51904520 | tf_op jit(solution)/shard_map/ppermute | solution.py:33
  260.1 146.7 %all-to-all-start = ((bf16[8,4,32768]{2,1,0:T(4,128)(2,1)}), bf16[8,4,32768]{2,1,0:T(4,128)(2,1)S(1)}, u32[]{:S(2)}, u32[]{:S(2)}) async-start(bf16[8,4,32768]{2,1,0:T(4,128)(2,1)} %reshape.5667), calls=%async_computation | async-start | bytes 4194304 | tf_op jit(solution)/shard_map/all_to_all | solution.py:285
  510.2 3.4 copy-start
  636.8 14.3 %all-to-all-start.1 = ((f32[8,1,216]{2,1,0:T(1,128)}), f32[8,1,216]{2,1,0:T(1,128)S(1)}, u32[]{:S(2)}, u32[]{:S(2)}) async-start(f32[8,1,216]{2,1,0:T(1,128)} %reshape.6287), calls=%async_computation.1 | async-start | bytes 16384 | tf_op jit(solution)/shard_map/all_to_all | solution.py:297
